TPU v7x, 256 devices: a whole 4x4x8 slice. The times are simulated.
256 devices in a mesh: dp: 32 (over x, y, core), tensor: 8 (over z).
Axes of the slice: x: 4, y: 4, z: 8, core: 2. Of those that a mesh axis runs over, the one named last changes fastest.
Arguments:
- layer_input: bfloat16 [65536, 4096], P('dp', 'tensor'), may hold values from -54 to 54
- queries: bfloat16 [65536, 2048], P('dp', 'tensor'), may hold values from -6 to 6
- keys_values: bfloat16 [65536, 2, 1024], P('dp', None, 'tensor'), may hold values from -6 to 6
- out_grads: bfloat16 [65536, 2048], P('dp', 'tensor'), may hold values from -6 to 6
- log_sums: bfloat16 [65536, 16], P('dp', 'tensor'), may hold values from 2.5 to 5.5
- deltas: bfloat16 [65536, 16], P('dp', 'tensor'), may hold values from -1.5 to 1.5
- tile_fill: int32 [32, 16], replicated, may hold values from 1 to 128, as said below
- tile_cont: int32 [32, 16], replicated, may hold values from 0 to 1, as said below
- moment_first: float32 [4096, 2, 1024], P(('tensor', 'dp')), may hold values from -2 to 2
- moment_second: float32 [2, 8], replicated, may hold values from 0.05 to 0.5
Outputs:
- update: float32 [4096, 2, 1024], P(('tensor', 'dp'))
- new_first: float32 [4096, 2, 1024], P(('tensor', 'dp'))
- new_second: float32 [2, 8], replicated
Inputs may be any that keep to these rules, and one draw needn't show every extreme that they name: `tile_fill`: a tile followed by a tile with tile_cont 1 has all 128 positions live. Documents span one or two tiles: tile_cont is 0 for the first tile of each group and never 1 for two tiles in a row.
All inputs are finite; a program needn't handle non-finite values.
Results may differ from a plain program's by a relative error of at most 0.0055.
Values may be sent and summed in bfloat16 or wider, within the bound.
No kernel may reach another device: no remote copies, remote signals or barrier semaphores. Data moves between devices by JAX's collectives and lax.ppermute only.
A program may use at most 64 MiB of HBM per device.

v0:
```python
import math

import jax
import jax.numpy as jnp
from jax import lax
from jax.sharding import Mesh
from jax.sharding import PartitionSpec as P

D = 4096
HD = 128
DP = ("dp_0", "dp_1", "dp_2")
TENSOR_DP = ("tensor", "dp_0", "dp_1", "dp_2")


ADAM_ONE = 0.9
ADAM_TWO = 0.95
ADAM_EPS = 1e-08


def split_up(array, dim, length):
    before, after = (array.shape[:dim], array.shape[dim + 1 :])
    return jnp.moveaxis(array.reshape(*before, length, -1, *after), dim, 0)


def sum_at_owner(array, axis, dim):
    parts = split_up(array, dim, lax.axis_size(axis))
    arrived = lax.all_to_all(parts, axis, split_axis=0, concat_axis=0, tiled=True)
    return arrived.astype(jnp.float32).sum(axis=0)


def summed_rows(array, axes, dim):
    far, near = axes
    parts = split_up(array, dim, lax.axis_size(far))
    nearer = sum_at_owner(parts, near, dim + 1)
    arrived = lax.all_to_all(
        nearer.astype(jnp.bfloat16), far, split_axis=0, concat_axis=0, tiled=True
    )
    return arrived.astype(jnp.float32).sum(axis=0)


def sent_to_all(array, axis):
    length = lax.axis_size(axis)
    return lax.all_to_all(
        jnp.broadcast_to(array[None], (length, *array.shape)), axis, 0, 0, tiled=True
    )


def taken_together(array, axis):
    everything = sent_to_all(array, axis)
    return jnp.sum(everything, axis=0)


def one_axis_at_a_time(array, axes):
    far, near = axes
    return taken_together(taken_together(array, near), far)


def band_grads(q_tiles, k_tiles, v_tiles, do_tiles, lse_tiles, delta_tiles, fill_tiles, cont_tiles):
    tile_total, block_len, groups, head_width = q_tiles.shape
    scale_qk = head_width ** (-0.5)
    zero_tile = jnp.zeros_like(k_tiles[:1])
    k_window = jnp.concatenate([jnp.concatenate([zero_tile, k_tiles[:-1]], 0), k_tiles], 1)
    v_window = jnp.concatenate([jnp.concatenate([zero_tile, v_tiles[:-1]], 0), v_tiles], 1)
    places = jnp.arange(block_len)
    live_rows = places[None, :] < fill_tiles[:, None]
    causal = places[:, None] >= places[None, :]
    own_part = live_rows[:, :, None] & causal[None]
    prev_part = (
        live_rows[:, :, None] & (cont_tiles[:, None, None] == 1) & (places[None, None, :] >= 0)
    )
    allowed = jnp.concatenate([prev_part, own_part], 2)[:, None]
    scores = (
        jnp.einsum("sqgd,skd->sgqk", q_tiles, k_window, preferred_element_type=jnp.float32)
        * scale_qk
    )
    lse_rows = jnp.swapaxes(lse_tiles.astype(jnp.float32), 1, 2)[..., None]
    delta_rows = jnp.swapaxes(delta_tiles.astype(jnp.float32), 1, 2)[..., None]
    prob_vals = jnp.where(allowed, jnp.exp(scores - lse_rows), 0.0)
    dprobs = jnp.einsum("sqgd,skd->sgqk", do_tiles, v_window, preferred_element_type=jnp.float32)
    dscores = prob_vals * (dprobs - delta_rows)
    value_grad = jnp.einsum(
        "sgqk,sqgd->skd",
        prob_vals.astype(jnp.bfloat16),
        do_tiles,
        preferred_element_type=jnp.float32,
    )
    key_grad = (
        jnp.einsum(
            "sgqk,sqgd->skd",
            dscores.astype(jnp.bfloat16),
            q_tiles,
            preferred_element_type=jnp.float32,
        )
        * scale_qk
    )
    key_out = key_grad[:, block_len:] + jnp.concatenate(
        [key_grad[1:, :block_len], jnp.zeros_like(key_grad[:1, :block_len])], 0
    )
    value_out = value_grad[:, block_len:] + jnp.concatenate(
        [value_grad[1:, :block_len], jnp.zeros_like(value_grad[:1, :block_len])], 0
    )
    return (key_out, value_out)


def attend_heads(q_tiles, kv_tiles, do_tiles, stat_tiles, fill_tiles, cont_tiles):
    tile_total, block_len = (q_tiles.shape[0], q_tiles.shape[1])
    kv_cols = kv_tiles.shape[3]
    kv_local = kv_cols // HD
    group_size = q_tiles.shape[2] // kv_cols
    q_heads = q_tiles.reshape(tile_total, block_len, kv_local, group_size, HD)
    do_heads = do_tiles.reshape(tile_total, block_len, kv_local, group_size, HD)
    stat_heads = stat_tiles.reshape(tile_total, block_len, 2, kv_local, group_size)
    key_out, value_out = band_grads(
        q_heads[:, :, 0],
        kv_tiles[:, :, 0, 0:HD],
        kv_tiles[:, :, 1, 0:HD],
        do_heads[:, :, 0],
        stat_heads[:, :, 0, 0],
        stat_heads[:, :, 1, 0],
        fill_tiles,
        cont_tiles,
    )
    results = jnp.stack([key_out, value_out], 2)
    return results.astype(jnp.bfloat16)


def per_device(
    layer_input,
    queries,
    keys_values,
    out_grads,
    log_sums,
    deltas,
    tile_fill,
    tile_cont,
    moment_first,
    moment_second,
):
    group_count = lax.axis_size(DP)
    tile_count = tile_fill.shape[1]
    token_count = queries.shape[0]
    block_len = token_count // tile_count
    my_group = lax.axis_index(DP)
    q_tiles = queries.reshape(tile_count, block_len, -1)
    kv_tiles = keys_values.reshape(tile_count, block_len, 2, -1)
    do_tiles = out_grads.reshape(tile_count, block_len, -1)
    stat_tiles = jnp.stack([log_sums, deltas], 1).reshape(tile_count, block_len, 2, -1)
    fill_mine = lax.dynamic_index_in_dim(tile_fill, my_group, 0, keepdims=False)
    cont_mine = lax.dynamic_index_in_dim(tile_cont, my_group, 0, keepdims=False)
    kv_grads = attend_heads(q_tiles, kv_tiles, do_tiles, stat_tiles, fill_mine, cont_mine)
    kv_grads = kv_grads.reshape(token_count, 2, -1)
    kv_every = lax.all_gather(kv_grads, "tensor", axis=2, tiled=True)
    summed = summed_rows(
        jnp.einsum("tr,tkc->rkc", layer_input, kv_every, preferred_element_type=jnp.float32).astype(
            jnp.bfloat16
        ),
        (("dp_0", "dp_1"), "dp_2"),
        0,
    )
    proj_grads = summed / math.sqrt(token_count * group_count)
    new_first = ADAM_ONE * moment_first + (1 - ADAM_ONE) * proj_grads
    heads_kv = moment_second.shape[1]
    partial_squares = jnp.sum(
        jnp.square(proj_grads).reshape(proj_grads.shape[0], 2, heads_kv, -1), axis=(0, 3)
    )
    squares = one_axis_at_a_time(partial_squares, (("dp_0", "dp_1"), ("dp_2", "tensor")))
    new_second = ADAM_TWO * moment_second + (1 - ADAM_TWO) * squares / (D * HD)
    step_size = jnp.sqrt(new_second / (1 - ADAM_TWO**2)) + ADAM_EPS
    scaled = (new_first / (1 - ADAM_ONE**2)).reshape(proj_grads.shape[0], 2, heads_kv, -1)
    update = (scaled / step_size[None, :, :, None]).reshape(proj_grads.shape)
    return (update, new_first, new_second)


def solution(mesh):
    split = Mesh(
        mesh.devices.reshape(4, 4, 2, mesh.shape["tensor"]), ("dp_0", "dp_1", "dp_2", "tensor")
    )
    placed = (
        P(DP, "tensor"),
        P(DP, "tensor"),
        P(DP, None, "tensor"),
        P(DP, "tensor"),
        P(DP, "tensor"),
        P(DP, "tensor"),
        P(),
        P(),
        P(TENSOR_DP, None, None),
        P(),
    )
    return jax.shard_map(
        per_device,
        mesh=split,
        in_specs=placed,
        out_specs=(P(TENSOR_DP, None, None), P(TENSOR_DP, None, None), P()),
        check_vma=False,
    )
```

profile of v0, /device:TPU:1, one launch (start us, length us, event | category | flops | bytes accessed | tf_op | source)
XLA Modules:
  0.0 207.2 jit_solution(17251893864657309062)
XLA Ops:
  7.2 0.0 copy-start
  7.2 0.0 all-gather.2.cloned.1.call-start
  7.3 1.5 copy.68
  8.8 0.0 copy-start.6
  8.8 0.0 copy-start.7
  8.8 1.1 slice_bitcast_fusion.2
  9.9 1.0 slice_bitcast_fusion
  10.9 0.0 copy-done.6
  10.9 0.2 dynamic-slice_reduce_fusion
  11.1 0.0 copy-done.7
  11.1 0.2 fusion.49
  11.3 0.0 copy-start.8
  11.3 0.0 copy-start.9
  11.3 1.4 squeeze_reshape_reshape.6
  12.7 2.2 %squeeze_reshape_reshape.7 = bf16[16,128,2,128]{3,2,1,0:T(2,128)(2,1)} reshape(bf16[2048,256]{1,0:T(8,128)(2,1)} %param.13) | data formatting | bytes 2097152 | tf_op jit(solution)/shard_map/squeeze;reshape;reshape | solution.py:117
  14.8 0.1 broadcast_and_fusion.1
  14.9 0.0 copy-done.8
  14.9 0.0 copy-done.9
  15.0 0.1 broadcast_and_fusion
  15.1 0.1 and.40
  15.2 0.0 copy-start.4
  15.2 0.0 copy-start.3
  15.3 2.1 %fusion.23 = f32[16,256,128,2]{2,1,3,0:T(8,128)S(1)} fusion(bf16[15,128,128]{2,1,0:T(8,128)(2,1)} %get-tuple-element.19, bf16[16,128,128]{2,1,0:T(8,128)(2,1)} %get-tuple-element.17, bf16[16,128,2,128]{3,2,1,0:T(2,128)(2,1)S(1)} %squeeze_reshape_reshape.6), kind=kOutput, calls=%fused_computation.25 | convolution fusion | flops 271581184 | bytes 6258688 | tf_op jit(solution)/shard_map/sqgd,skd->sgqk/dot_general | solution.py:73
  17.4 0.0 copy-start.1
  17.4 0.0 copy-done.4
  17.4 0.0 copy-done.3
  17.4 1.0 fusion.18
  18.5 0.8 copy-done.1
  19.3 0.1 slice.51
  19.4 1.0 fusion.29
  20.3 6.3 %bitcast_multiply_fusion = f32[16,256,128]{2,1,0:T(8,128)} fusion(f32[16,256,128,2]{2,1,3,0:T(8,128)} %copy-done.1, f32[16,2,128]{2,1,0:T(2,128)S(1)} %get-tuple-element.22, f32[16,2,128]{2,1,0:T(2,128)S(1)} %get-tuple-element.23, pred[16,128,256]{1,2,0:T(8,128)(4,1)} %copy-done.4, bf16[15,128,128]{2,1,0:T(8,128)(2,1)} %get-tuple-element.18, ...), kind=kOutput, calls=%fused_computation.13 | convolution fusion | flops 546832384 | bytes 9961472 | tf_op jit(solution)/shard_map/sgqk,sqgd->skd/dot_general | solution.py:88
  26.7 0.0 copy-start.2
  26.7 1.3 slice.49
  28.0 1.3 fusion.30
  29.3 0.0 copy-done.2
  29.3 1.2 pad_maximum_fusion
  30.5 0.0 all-gather.2.cloned.1.call-update
  30.5 101.6 %all-gather.2.cloned.1.call-done = bf16[2048,2,1024]{2,0,1:T(8,128)(2,1)} async-done(((bf16[2048,2,128]{2,0,1:T(8,128)(2,1)}), bf16[2048,2,1024]{2,0,1:T(8,128)(2,1)}) %all-gather.2.cloned.1.call-update) | async-done | bytes 8388624 | tf_op jit(solution)/shard_map/all_gather | solution.py:152
  132.1 0.0 copy-done
  132.1 8.2 %fusion.15 = bf16[2,1024,512]{1,2,0:T(8,128)(2,1)S(1)} fusion(bf16[2048,2,1024]{2,0,1:T(8,128)(2,1)} %all-gather.2.cloned.1.call-done, bf16[2048,512]{1,0:T(8,128)(2,1)S(1)} %copy-done), kind=kOutput, calls=%fused_computation.21 | convolution fusion | flops 4296015872 | bytes 12582912 | tf_op jit(solution)/shard_map/tr,tkc->rkc/dot_general | solution.py:154
  140.3 0.3 copy.112
  140.6 9.9 %all_to_all.20 = bf16[2,16,16,2,1024]{4,2,1,3,0:T(8,128)(2,1)} all-to-all(bf16[2,16,16,2,1024]{4,2,1,3,0:T(8,128)(2,1)S(1)} %bitcast.83), channel_id=1, replica_groups=mesh['dp_0'=4,'dp_1'=4,'dp_2'=2,'tensor'=8] {'dp_2'}, dimensions={0} | all-to-all | bytes 4194304 | tf_op jit(solution)/shard_map/all_to_all | solution.py:27
  150.5 2.2 %reduce_sum.55 = bf16[16,16,2,1024]{3,1,0,2:T(8,128)(2,1)S(1)} reduce(bf16[2,16,16,2,1024]{4,2,1,3,0:T(8,128)(2,1)} %all_to_all.20, bf16[]{:T(256)} %constant.53.clone.1), dimensions={0}, to_apply=%region_0.1 | reduce | flops 524288 | bytes 3145730 | tf_op jit(solution)/shard_map/reduce_sum | solution.py:28
  152.7 0.1 copy.78
  152.8 0.0 copy-start.10
  152.8 0.0 copy-start.5
  152.8 22.4 %all_to_all.21 = bf16[16,16,2,1024]{3,1,2,0:T(8,128)(2,1)S(1)} all-to-all(bf16[16,16,2,1024]{3,1,2,0:T(8,128)(2,1)S(1)} %copy.78), channel_id=1, replica_groups=mesh['dp_0'=4,'dp_1'=4,'dp_2'=2,'tensor'=8] {'dp_0','dp_1'}, dimensions={0} | all-to-all | bytes 2097152 | tf_op jit(solution)/shard_map/all_to_all | solution.py:35
  175.3 0.2 convert_reduce_fusion
  175.5 0.1 bitcast_reduce_fusion
  175.6 13.0 %all_to_all.22 = f32[16,2,8]{2,1,0:T(2,128)S(1)} all-to-all(f32[16,2,8]{2,1,0:T(2,128)S(1)} %broadcast_in_dim.14), channel_id=1, replica_groups=mesh['dp_0'=4,'dp_1'=4,'dp_2'=2,'tensor'=8] {'dp_2','tensor'}, dimensions={0} | all-to-all | bytes 2048 | tf_op jit(solution)/shard_map/all_to_all | solution.py:43
  188.7 9.4 %all_to_all.23 = f32[16,2,8]{2,1,0:T(2,128)S(1)} all-to-all(f32[16,2,8]{2,1,0:T(2,128)S(1)} %broadcast_in_dim.15), channel_id=1, replica_groups=mesh['dp_0'=4,'dp_1'=4,'dp_2'=2,'tensor'=8] {'dp_0','dp_1'}, dimensions={0} | all-to-all | bytes 2048 | tf_op jit(solution)/shard_map/all_to_all | solution.py:43
  198.1 0.0 copy-done.10
  198.1 0.6 sqrt_add_fusion
  198.7 0.1 broadcast_bitcast_fusion
  198.8 0.0 copy-done.5
  198.8 0.1 multiply_divide_fusion
  198.9 0.8 copy.82
  199.6 0.8 copy.83
  (9 shorter events, 0.2 us)
Async XLA Ops:
  7.2 125.0 %copy-start = (bf16[2048,512]{1,0:T(8,128)(2,1)S(1)}, bf16[2048,512]{1,0:T(8,128)(2,1)}, u32[]{:S(2)}) copy-start(bf16[2048,512]{1,0:T(8,128)(2,1)} %param.10) | copy-start | bytes 6291460
  7.2 125.0 %all-gather.2.cloned.1.call-start = ((), (), s32[]{:S(2)}) async-start(), calls=%async_computation.4 | async-start | bytes 9437184 | tf_op jit(solution)/shard_map/all_gather | solution.py:152
  8.8 2.2 %copy-start.6 = (s32[32,16]{0,1:T(8,128)S(1)}, s32[32,16]{0,1:T(8,128)}, u32[]{:S(2)}) copy-start(s32[32,16]{0,1:T(8,128)} %param.16) | copy-start | bytes 6148
  8.8 2.3 %copy-start.7 = (s32[32,16]{0,1:T(8,128)S(1)}, s32[32,16]{0,1:T(8,128)}, u32[]{:S(2)}) copy-start(s32[32,16]{0,1:T(8,128)} %param.17) | copy-start | bytes 6148
  11.3 3.6 %copy-start.8 = (bf16[2048,2]{0,1:T(2,128)(2,1)S(1)}, bf16[2048,2]{0,1:T(2,128)(2,1)}, u32[]{:S(2)}) copy-start(bf16[2048,2]{0,1:T(2,128)(2,1)} %param.15) | copy-start | bytes 24580
  11.3 3.6 %copy-start.9 = (bf16[2048,2]{0,1:T(2,128)(2,1)S(1)}, bf16[2048,2]{0,1:T(2,128)(2,1)}, u32[]{:S(2)}) copy-start(bf16[2048,2]{0,1:T(2,128)(2,1)} %param.14) | copy-start | bytes 24580
  15.2 2.1 %copy-start.4 = (pred[16,128,256]{1,2,0:T(8,128)(4,1)}, pred[16,128,256]{1,2,0:T(8,128)(4,1)S(1)}, u32[]{:S(2)}) copy-start(pred[16,128,256]{1,2,0:T(8,128)(4,1)S(1)} %pad_add_fusion) | copy-start | bytes 1572868
  15.2 2.1 %copy-start.3 = (bf16[16,128,2,128]{3,2,1,0:T(2,128)(2,1)S(1)}, bf16[16,128,2,128]{3,2,1,0:T(2,128)(2,1)}, u32[]{:S(2)}) copy-start(bf16[16,128,2,128]{3,2,1,0:T(2,128)(2,1)} %squeeze_reshape_reshape.7) | copy-start | bytes 3145732
  17.4 1.9 copy-start.1
  26.7 2.7 %copy-start.2 = (bf16[16,128,128]{2,1,0:T(8,128)(2,1)S(1)}, bf16[16,128,128]{2,1,0:T(8,128)(2,1)}, u32[]{:S(2)}) copy-start(bf16[16,128,128]{2,1,0:T(8,128)(2,1)} %fusion.29) | copy-start | bytes 1572868
  152.8 45.3 %copy-start.10 = (f32[2,8]{1,0:T(2,128)S(1)}, f32[2,8]{1,0:T(2,128)}, u32[]{:S(2)}) copy-start(f32[2,8]{1,0:T(2,128)} %param.19) | copy-start | bytes 196
  152.8 45.9 %copy-start.5 = (f32[16,2,1024]{2,1,0:T(2,128)S(1)}, f32[16,2,1024]{2,1,0:T(2,128)}, u32[]{:S(2)}) copy-start(f32[16,2,1024]{2,1,0:T(2,128)} %param.18) | copy-start | bytes 393220
Sparse Core Ops, SparseCore 0:
  30.7 101.4 all-gather.1
where the time goes:
time: 208 us; the launch traced here: 207 us
  waiting for transfers between devices  102 us (49%)
  blocking collectives  54.8 us (26%)
  matrix products  17.6 us (8%)
  between operations  14.3 us (7%)
  local copies, waits for them, and re-layouts  11.7 us (6%)
  other arithmetic  7.15 us (3%)
    all_gather x1, waiting for transfers between devices, per_device(): kv_every = lax.all_gather(kv_grads, 'tensor', axis=2, tiled=True)  102 us
    all_to_all x2, blocking collectives, sent_to_all(): lax.all_to_all(jnp.broadcast_to(array[None], (length, *array.shape)), axi...  22.5 us
    all_to_all x1, blocking collectives, summed_rows(): lax.all_to_all(nearer.astype(jnp.bfloat16), far, split_axis=0, concat_axi...  22.4 us
    all_to_all x1, blocking collectives, sum_at_owner(): lax.all_to_all(parts, axis, split_axis=0, concat_axis=0, tiled=True)  9.87 us
    dot_general x1, matrix products, per_device(): jnp.einsum('tr,tkc->rkc', layer_input, kv_every, preferred_element_type=j...  8.16 us
    dot_general x1, matrix products, band_grads(): jnp.einsum('sgqk,sqgd->skd', dscores.astype(jnp.bfloat16), q_tiles, prefe...  6.33 us
  transfers between devices with their start and end apart: 1, of which 1 were waited for; matrix products, arithmetic and copies ran while one was open for 0% of the time, Pallas kernels for 0%

commit v1 on v0

v1 whole, which is shorter than its diff:
```python
import functools
import math

import jax
import jax.numpy as jnp
from jax import lax
from jax.experimental import pallas as pl
from jax.experimental.pallas import tpu as pltpu
from jax.sharding import Mesh
from jax.sharding import PartitionSpec as P

D = 4096
HD = 128
BLK = 128
DP = ("dp_0", "dp_1", "dp_2")
TENSOR_DP = ("tensor", "dp_0", "dp_1", "dp_2")

ADAM_ONE = 0.9
ADAM_TWO = 0.95
ADAM_EPS = 1e-08

NT = (((1,), (1,)), ((), ()))
NN = (((1,), (0,)), ((), ()))
TN = (((0,), (0,)), ((), ()))


def attention_kernel(
    first,
    per_step,
    tile_count,
    fill_ref,
    cont_ref,
    q_ref,
    q_next_ref,
    do_ref,
    do_next_ref,
    kv_ref,
    lse_ref,
    lse_next_ref,
    delta_ref,
    delta_next_ref,
    out_ref,
):
    heads = q_ref.shape[1] // HD
    scale_qk = HD ** (-0.5)
    base = first + pl.program_id(0) * per_step
    for j in range(per_step):
        tile = base + j
        rows = pl.ds(j * BLK, BLK)
        after = jnp.minimum(tile + 1, tile_count - 1)
        fill_own = fill_ref[tile]
        linked = jnp.where(tile + 1 < tile_count, cont_ref[after], 0)
        fill_next = jnp.where(linked == 1, fill_ref[after], 0)

        def window(ref, next_ref, h):
            columns = slice(h * HD, (h + 1) * HD)
            own = ref[rows, columns]
            if j + 1 < per_step:
                follow = ref[pl.ds((j + 1) * BLK, BLK), columns]
            else:
                follow = next_ref[:, columns]
            return [own, follow]

        def stat(ref, next_ref, h):
            own = ref[h : h + 1, pl.ds(j * BLK, BLK)]
            if j + 1 < per_step:
                follow = ref[h : h + 1, pl.ds((j + 1) * BLK, BLK)]
            else:
                follow = next_ref[h : h + 1, :]
            return [own.astype(jnp.float32), follow.astype(jnp.float32)]

        def stack(pick, ref, next_ref, axis):
            return jnp.concatenate(sum([pick(ref, next_ref, h) for h in range(heads)], []), axis)

        q_all = stack(window, q_ref, q_next_ref, 0)
        do_all = stack(window, do_ref, do_next_ref, 0)
        lse_row = stack(stat, lse_ref, lse_next_ref, 1)
        delta_row = stack(stat, delta_ref, delta_next_ref, 1)
        keys = kv_ref[0, rows, :]
        values = kv_ref[1, rows, :]
        scores = lax.dot_general(keys, q_all, NT, preferred_element_type=jnp.float32) * scale_qk
        dprobs = lax.dot_general(values, do_all, NT, preferred_element_type=jnp.float32)
        key_place = lax.broadcasted_iota(jnp.int32, (BLK, BLK), 0)
        query_place = lax.broadcasted_iota(jnp.int32, (BLK, BLK), 1)
        own_part = (query_place < fill_own) & (query_place >= key_place)
        next_part = query_place < fill_next
        allowed = jnp.concatenate([own_part, next_part] * heads, 1)
        probs = jnp.where(allowed, jnp.exp(scores - lse_row), 0.0)
        dscores = probs * (dprobs - delta_row)
        value_grad = lax.dot_general(
            probs.astype(jnp.bfloat16), do_all, NN, preferred_element_type=jnp.float32
        )
        key_grad = (
            lax.dot_general(
                dscores.astype(jnp.bfloat16), q_all, NN, preferred_element_type=jnp.float32
            )
            * scale_qk
        )
        out_ref[rows, 0:HD] = key_grad.astype(jnp.bfloat16)
        out_ref[rows, HD : 2 * HD] = value_grad.astype(jnp.bfloat16)


def attention(first, count, per_step, fill, cont, queries, out_grads, keys_values, lse, delta):
    tile_count = queries.shape[0] // BLK
    width = queries.shape[1]
    steps = count // per_step
    offset = first // per_step

    def own(i, *_):
        return (offset + i, 0)

    def follow(i, *_):
        return (jnp.minimum(first + (i + 1) * per_step, tile_count - 1), 0)

    def own_lanes(i, *_):
        return (0, offset + i)

    def follow_lanes(i, *_):
        return (0, jnp.minimum(first + (i + 1) * per_step, tile_count - 1))

    rows = per_step * BLK
    heads = lse.shape[0]
    return pl.pallas_call(
        functools.partial(attention_kernel, first, per_step, tile_count),
        grid_spec=pltpu.PrefetchScalarGridSpec(
            num_scalar_prefetch=2,
            grid=(steps,),
            in_specs=[
                pl.BlockSpec((rows, width), own),
                pl.BlockSpec((BLK, width), follow),
                pl.BlockSpec((rows, width), own),
                pl.BlockSpec((BLK, width), follow),
                pl.BlockSpec((2, rows, HD), lambda i, *_: (0, offset + i, 0)),
                pl.BlockSpec((heads, rows), own_lanes),
                pl.BlockSpec((heads, BLK), follow_lanes),
                pl.BlockSpec((heads, rows), own_lanes),
                pl.BlockSpec((heads, BLK), follow_lanes),
            ],
            out_specs=pl.BlockSpec((rows, 2 * HD), lambda i, *_: (i, 0)),
        ),
        out_shape=jax.ShapeDtypeStruct((count * BLK, 2 * HD), jnp.bfloat16),
        compiler_params=pltpu.CompilerParams(vmem_limit_bytes=32 * 1024 * 1024),
        cost_estimate=pl.CostEstimate(
            flops=count * 8 * heads * BLK * 2 * BLK * HD,
            bytes_accessed=count * BLK * 10 * HD * 2,
            transcendentals=count * heads * 2 * BLK * BLK,
        ),
        name="attention_grads",
    )(fill, cont, queries, queries, out_grads, out_grads, keys_values, lse, lse, delta, delta)


def shifted(array, steps, length):
    return lax.ppermute(array, "tensor", [(i, (i + steps) % length) for i in range(length)])


def sum_at_owner(block, axes):
    length = lax.axis_size(axes)
    parts = block.reshape(length, -1, block.shape[1])
    arrived = lax.all_to_all(parts, axes, split_axis=0, concat_axis=0, tiled=True)
    return arrived.astype(jnp.float32).sum(axis=0)


def taken_together(array, axes):
    length = lax.axis_size(axes)
    everything = lax.all_to_all(
        jnp.broadcast_to(array[None], (length, *array.shape)), axes, 0, 0, tiled=True
    )
    return jnp.sum(everything, axis=0)


def per_device(
    layer_input,
    queries,
    keys_values,
    out_grads,
    log_sums,
    deltas,
    tile_fill,
    tile_cont,
    moment_first,
    moment_second,
):
    group_count = lax.axis_size(DP)
    ring = lax.axis_size("tensor")
    tile_count = tile_fill.shape[1]
    token_count = queries.shape[0]
    my_group = lax.axis_index(DP)
    place = lax.axis_index("tensor")
    fill = lax.dynamic_index_in_dim(tile_fill, my_group, 0, keepdims=False)
    cont = lax.dynamic_index_in_dim(tile_cont, my_group, 0, keepdims=False)
    kv = jnp.swapaxes(keys_values, 0, 1)
    half = tile_count // 2
    halves = [
        attention(first, half, 4, fill, cont, queries, out_grads, kv, log_sums.T, deltas.T)
        for first in (0, half)
    ]
    inputs = [layer_input[: half * BLK], layer_input[half * BLK :]]

    blocks = {0: list(halves)}
    right, left = list(halves), list(halves)
    far = ring // 2
    for step in range(1, far):
        for part in range(2):
            right[part] = shifted(right[part], 1, ring)
            left[part] = shifted(left[part], -1, ring)
        blocks[-step] = list(right)
        blocks[step] = list(left)
    blocks[far] = [shifted(right[0], 1, ring), shifted(left[1], -1, ring)]

    def product(offset):
        one, two = (
            lax.dot_general(x, b, TN, preferred_element_type=jnp.float32)
            for x, b in zip(inputs, blocks[offset])
        )
        return (one + two).astype(jnp.bfloat16)

    summed = {}
    for offsets in ((0, -1, 1), (-2, 2), (-3, 3, far)):
        together = jnp.concatenate([product(o) for o in offsets], 1)
        total = sum_at_owner(together, DP)
        for i, o in enumerate(offsets):
            summed[o % ring] = total[:, i * 2 * HD : (i + 1) * 2 * HD]

    rows = moment_first.shape[0]
    in_turn = jnp.stack([summed[o].reshape(rows, 2, HD) for o in range(ring)], 2)
    twice = jnp.concatenate([in_turn, in_turn], 2)
    ordered = lax.dynamic_slice_in_dim(twice, (ring - place) % ring, ring, 2)
    proj_grads = ordered.reshape(rows, 2, -1) / math.sqrt(token_count * group_count)

    new_first = ADAM_ONE * moment_first + (1 - ADAM_ONE) * proj_grads
    heads_kv = moment_second.shape[1]
    partial_squares = jnp.sum(
        jnp.square(proj_grads).reshape(rows, 2, heads_kv, -1), axis=(0, 3)
    )
    squares = taken_together(taken_together(partial_squares, DP), ("tensor",))
    new_second = ADAM_TWO * moment_second + (1 - ADAM_TWO) * squares / (D * HD)
    step_size = jnp.sqrt(new_second / (1 - ADAM_TWO**2)) + ADAM_EPS
    scaled = (new_first / (1 - ADAM_ONE**2)).reshape(rows, 2, heads_kv, -1)
    update = (scaled / step_size[None, :, :, None]).reshape(proj_grads.shape)
    return (update, new_first, new_second)


def solution(mesh):
    split = Mesh(
        mesh.devices.reshape(4, 4, 2, mesh.shape["tensor"]), ("dp_0", "dp_1", "dp_2", "tensor")
    )
    placed = (
        P(DP, "tensor"),
        P(DP, "tensor"),
        P(DP, None, "tensor"),
        P(DP, "tensor"),
        P(DP, "tensor"),
        P(DP, "tensor"),
        P(),
        P(),
        P(TENSOR_DP, None, None),
        P(),
    )
    return jax.shard_map(
        per_device,
        mesh=split,
        in_specs=placed,
        out_specs=(P(TENSOR_DP, None, None), P(TENSOR_DP, None, None), P()),
        check_vma=False,
    )
```

time: 208 us -> 153 us (0.74)
  starting transfers between devices: 0.04 us -> 51.7 us
  waiting for transfers between devices: 102 us -> 54.7 us
  blocking collectives: 54.8 us -> 10.9 us
  between operations: 14.3 us -> 1.11 us
  Pallas kernels: 0 us -> 5.52 us
  other arithmetic: 7.15 us -> 2.05 us
  local copies, waits for them, and re-layouts: 11.7 us -> 7.34 us
    all_gather x1 -> x0, waiting for transfers between devices: 102 us -> none  [per_device(): kv_every = lax.all_gather(kv_grads, 'tensor', axis=2, tiled=True)]
    all_to_all x4 -> x1, blocking collectives: 54.8 us -> 10.9 us  [taken_together(): lax.all_to_all(jnp.broadcast_to(array[None], (length, *array.shape)), axe...]
    ppermute x0 -> x14, waiting for transfers between devices: none -> 29.3 us  [shifted(): lax.ppermute(array, 'tensor', [(i, (i + steps) % length) for i in range(l...]
    all_to_all x0 -> x4, starting transfers between devices: none -> 27.6 us  [the longest x3 23.1 us: sum_at_owner(): lax.all_to_all(parts, axes, split_axis=0, concat_axis=0, tiled=True)]
    all_to_all x0 -> x4, waiting for transfers between devices: none -> 25.4 us  [the longest x3 18.9 us: sum_at_owner(): lax.all_to_all(parts, axes, split_axis=0, concat_axis=0, tiled=True)]
    ppermute x0 -> x14, starting transfers between devices: none -> 24.1 us  [shifted(): lax.ppermute(array, 'tensor', [(i, (i + steps) % length) for i in range(l...]
    pallas_call x0 -> x2, Pallas kernels: none -> 5.52 us  [attention(): pl.pallas_call(functools.partial(attention_kernel, first, per_step, tile_...]
    concatenate x0 -> x4, local copies, waits for them, and re-layouts: none -> 3.73 us  [the longest x3 3.34 us: per_device(): together = jnp.concatenate([product(o) for o in offsets], 1)]
  transfers between devices with their start and end apart: 1 -> 18, of which waited for: 1 -> 11; matrix products, arithmetic and copies ran while one was open for 0% -> 15% of each run, Pallas kernels for 0% -> 2%
where the time goes in v1:
time: 153 us; the launch traced here: 152 us
  waiting for transfers between devices  54.7 us (36%)
  starting transfers between devices  51.7 us (34%)
  matrix products  19.1 us (12%)
  blocking collectives  10.9 us (7%)
  local copies, waits for them, and re-layouts  7.34 us (5%)
  Pallas kernels  5.52 us (4%)
  other arithmetic  2.05 us (1%)
    ppermute x14, waiting for transfers between devices, shifted(): lax.ppermute(array, 'tensor', [(i, (i + steps) % length) for i in range(l...  29.3 us
    ppermute x14, starting transfers between devices, shifted(): lax.ppermute(array, 'tensor', [(i, (i + steps) % length) for i in range(l...  24.1 us
    all_to_all x3, starting transfers between devices, sum_at_owner(): lax.all_to_all(parts, axes, split_axis=0, concat_axis=0, tiled=True)  23.1 us
    dot_general x16, matrix products, product(): lax.dot_general(x, b, TN, preferred_element_type=jnp.float32)  19.1 us
    all_to_all x3, waiting for transfers between devices, sum_at_owner(): lax.all_to_all(parts, axes, split_axis=0, concat_axis=0, tiled=True)  18.9 us
    all_to_all x1, blocking collectives, taken_together(): lax.all_to_all(jnp.broadcast_to(array[None], (length, *array.shape)), axe...  10.9 us
    all_to_all x1, waiting for transfers between devices, taken_together(): lax.all_to_all(jnp.broadcast_to(array[None], (length, *array.shape)), axe...  6.5 us
    pallas_call x2, Pallas kernels, attention(): pl.pallas_call(functools.partial(attention_kernel, first, per_step, tile_...  5.52 us
  transfers between devices with their start and end apart: 18, of which 11 were waited for; matrix products, arithmetic and copies ran while one was open for 15% of the time, Pallas kernels for 2%

profile of v1, /device:TPU:1, one launch (start us, length us, event | category | flops | bytes accessed | tf_op | source)
XLA Modules:
  0.0 152.5 jit_solution(9490874466808733474)
XLA Ops:
  0.7 1.5 copy.33
  2.2 0.2 dynamic-slice_reduce_fusion
  2.4 0.1 copy-done.1
  2.5 2.8 %attention_grads.3 = bf16[1024,256]{1,0:T(8,128)(2,1)S(1)} custom-call(s32[16]{0:T(128)S(1)} %get-tuple-element.18.fill_ref, s32[16]{0:T(128)S(1)} %get-tuple-element.17.cont_ref, bf16[2048,256]{1,0:T(8,128)(2,1)S(1)} %copy-done, bf16[2048,256]{1,0:T(8,128)(2,1)S(1)} %copy-done, bf16[2048,256]{1,0:T(8,128)(2,1)S(1)} %copy-done.1, ...), custom_call_target="tpu_custom_call" | custom-call | flops 536870912 | bytes 2621440 | tf_op jit(solution)/shard_map/attention_grads/pallas_call | solution.py:123
  5.3 0.0 copy-start.8
  5.3 6.5 %collective-permute-start.3 = (bf16[1024,256]{1,0:T(8,128)(2,1)S(1)}, bf16[1024,256]{1,0:T(8,128)(2,1)}, u32[]{:S(2)}, u32[]{:S(2)}) collective-permute-start(bf16[1024,256]{1,0:T(8,128)(2,1)S(1)} %attention_grads.3), channel_id=1, source_target_pairs={{0,7},{1,0},{2,1},{3,2},{4,3},{5,4},{6,5},{7,6},{8,15},{9,8},{10,9... | collective-permute-start | bytes 1572872 | tf_op jit(solution)/shard_map/ppermute | solution.py:153
  11.8 2.8 %attention_grads.2 = bf16[1024,256]{1,0:T(8,128)(2,1)S(1)} custom-call(s32[16]{0:T(128)S(1)} %get-tuple-element.18.fill_ref, s32[16]{0:T(128)S(1)} %get-tuple-element.17.cont_ref, bf16[2048,256]{1,0:T(8,128)(2,1)S(1)} %copy-done, bf16[2048,256]{1,0:T(8,128)(2,1)S(1)} %copy-done, bf16[2048,256]{1,0:T(8,128)(2,1)S(1)} %copy-done.1, ...), custom_call_target="tpu_custom_call" | custom-call | flops 536870912 | bytes 2621440 | tf_op jit(solution)/shard_map/attention_grads/pallas_call | solution.py:123
  14.5 2.8 %collective-permute-start.2 = (bf16[1024,256]{1,0:T(8,128)(2,1)S(1)}, bf16[1024,256]{1,0:T(8,128)(2,1)S(1)}, u32[]{:S(2)}, u32[]{:S(2)}) collective-permute-start(bf16[1024,256]{1,0:T(8,128)(2,1)S(1)} %attention_grads.2), channel_id=1, source_target_pairs={{0,7},{1,0},{2,1},{3,2},{4,3},{5,4},{6,5},{7,6},{8,15},{9,8},{10,9... | collective-permute-start | bytes 1572872 | tf_op jit(solution)/shard_map/ppermute | solution.py:153
  17.3 0.4 fusion.38
  17.8 0.5 fusion.15
  18.2 4.1 %collective-permute-done.3 = bf16[1024,256]{1,0:T(8,128)(2,1)} collective-permute-done((bf16[1024,256]{1,0:T(8,128)(2,1)S(1)}, bf16[1024,256]{1,0:T(8,128)(2,1)}, u32[]{:S(2)}, u32[]{:S(2)}) %collective-permute-start.3) | collective-permute-done | bytes 524320 | tf_op jit(solution)/shard_map/ppermute | solution.py:153
  22.3 3.5 %collective-permute-start.7 = (bf16[1024,256]{1,0:T(8,128)(2,1)}, bf16[1024,256]{1,0:T(8,128)(2,1)}, u32[]{:S(2)}, u32[]{:S(2)}) collective-permute-start(bf16[1024,256]{1,0:T(8,128)(2,1)} %collective-permute-done.3), channel_id=1, source_target_pairs={{0,7},{1,0},{2,1},{3,2},{4,3},{5,4},{6,5},{7,6},{8,15},{9,8},{10,9... | collective-permute-start | bytes 1572872 | tf_op jit(solution)/shard_map/ppermute | solution.py:153
  25.9 1.5 fusion.28
  27.4 9.4 %collective-permute-done = bf16[1024,256]{1,0:T(8,128)(2,1)} collective-permute-done((bf16[1024,256]{1,0:T(8,128)(2,1)S(1)}, bf16[1024,256]{1,0:T(8,128)(2,1)}, u32[]{:S(2)}, u32[]{:S(2)}) %collective-permute-start) | collective-permute-done | bytes 524320 | tf_op jit(solution)/shard_map/ppermute | solution.py:153
  36.8 1.5 %fusion.14 = bf16[512,256]{0,1:T(8,128)(2,1)S(1)} fusion(f32[256,512]{1,0:T(8,128)S(1)} %fusion.28, bf16[1024,256]{1,0:T(8,128)(2,1)} %collective-permute-done, bf16[2048,512]{1,0:T(8,128)(2,1)S(1)} %copy-done.8), kind=kOutput, calls=%fused_computation.24 | convolution fusion | flops 268697600 | bytes 2359296 | tf_op jit(solution)/shard_map/dot_general | solution.py:212
  38.3 1.5 fusion.26
  39.8 0.5 fusion.13
  40.3 0.0 copy-start.9
  40.3 0.1 pad_maximum_fusion
  40.4 1.2 copy.23
  41.5 10.5 %all-to-all-start = ((bf16[32,16,768]{2,1,0:T(8,128)(2,1)}), bf16[32,16,768]{2,1,0:T(8,128)(2,1)S(1)}, u32[]{:S(2)}, u32[]{:S(2)}) async-start(bf16[32,16,768]{2,1,0:T(8,128)(2,1)} %bitcast.6), calls=%async_computation | async-start | bytes 1572864 | tf_op jit(solution)/shard_map/all_to_all | solution.py:159
  52.0 3.0 %collective-permute-start.6 = (bf16[1024,256]{1,0:T(8,128)(2,1)S(1)}, bf16[1024,256]{1,0:T(8,128)(2,1)S(1)}, u32[]{:S(2)}, u32[]{:S(2)}) collective-permute-start(bf16[1024,256]{1,0:T(8,128)(2,1)S(1)} %collective-permute-done.2), channel_id=1, source_target_pairs={{0,7},{1,0},{2,1},{3,2},{4,3},{5,4},{6,5},{7,6},{8,15},{9,8},{10,9... | collective-permute-start | bytes 1572872 | tf_op jit(solution)/shard_map/ppermute | solution.py:153
  55.0 0.1 collective-permute-start.11
  55.1 1.4 collective-permute-start.9
  56.5 1.5 fusion.24
  58.0 1.2 collective-permute-done.4
  59.2 1.5 %fusion.12 = bf16[512,256]{0,1:T(8,128)(2,1)S(1)} fusion(f32[256,512]{1,0:T(8,128)S(1)} %fusion.24, bf16[1024,256]{1,0:T(8,128)(2,1)} %collective-permute-done.4, bf16[2048,512]{1,0:T(8,128)(2,1)S(1)} %copy-done.9), kind=kOutput, calls=%fused_computation.22 | convolution fusion | flops 268697600 | bytes 2359296 | tf_op jit(solution)/shard_map/dot_general | solution.py:212
  60.8 1.5 fusion.22
  62.3 3.8 %collective-permute-done.6 = bf16[1024,256]{1,0:T(8,128)(2,1)S(1)} collective-permute-done((bf16[1024,256]{1,0:T(8,128)(2,1)S(1)}, bf16[1024,256]{1,0:T(8,128)(2,1)S(1)}, u32[]{:S(2)}, u32[]{:S(2)}) %collective-permute-start.6) | collective-permute-done | bytes 524320 | tf_op jit(solution)/shard_map/ppermute | solution.py:153
  66.1 0.8 copy-done.12
  66.9 0.5 fusion.11
  67.4 1.0 copy.24
  68.4 3.4 %collective-permute-start.10 = (bf16[1024,256]{1,0:T(8,128)(2,1)}, bf16[1024,256]{1,0:T(8,128)(2,1)S(1)}, u32[]{:S(2)}, u32[]{:S(2)}) collective-permute-start(bf16[1024,256]{1,0:T(8,128)(2,1)} %copy-done.12), channel_id=1, source_target_pairs={{0,7},{1,0},{2,1},{3,2},{4,3},{5,4},{6,5},{7,6},{8,15},{9,8},{10,9... | collective-permute-start | bytes 1572872 | tf_op jit(solution)/shard_map/ppermute | solution.py:153
  71.8 5.6 %collective-permute-done.11 = bf16[1024,256]{1,0:T(8,128)(2,1)} collective-permute-done((bf16[1024,256]{1,0:T(8,128)(2,1)}, bf16[1024,256]{1,0:T(8,128)(2,1)}, u32[]{:S(2)}, u32[]{:S(2)}) %collective-permute-start.11) | collective-permute-done | bytes 524320 | tf_op jit(solution)/shard_map/ppermute | solution.py:153
  77.4 3.4 %collective-permute-start.13 = (bf16[1024,256]{1,0:T(8,128)(2,1)}, bf16[1024,256]{1,0:T(8,128)(2,1)}, u32[]{:S(2)}, u32[]{:S(2)}) collective-permute-start(bf16[1024,256]{1,0:T(8,128)(2,1)} %collective-permute-done.11), channel_id=1, source_target_pairs={{0,7},{1,0},{2,1},{3,2},{4,3},{5,4},{6,5},{7,6},{8,15},{9,8},{10,9... | collective-permute-start | bytes 1572872 | tf_op jit(solution)/shard_map/ppermute | solution.py:153
  80.9 1.2 collective-permute-done.8
  82.1 1.5 fusion.20
  83.6 1.5 fusion.10
  85.1 1.5 fusion.18
  86.6 2.1 %collective-permute-done.10 = bf16[1024,256]{1,0:T(8,128)(2,1)S(1)} collective-permute-done((bf16[1024,256]{1,0:T(8,128)(2,1)}, bf16[1024,256]{1,0:T(8,128)(2,1)S(1)}, u32[]{:S(2)}, u32[]{:S(2)}) %collective-permute-start.10) | collective-permute-done | bytes 524320 | tf_op jit(solution)/shard_map/ppermute | solution.py:153
  88.7 0.5 fusion.9
  89.2 8.9 %all-to-all-start.1 = ((bf16[32,16,512]{2,1,0:T(8,128)(2,1)}), bf16[32,16,512]{2,1,0:T(8,128)(2,1)S(1)}, u32[]{:S(2)}, u32[]{:S(2)}) async-start(bf16[32,16,512]{2,1,0:T(8,128)(2,1)} %bitcast.9), calls=%async_computation.1 | async-start | bytes 1048576 | tf_op jit(solution)/shard_map/all_to_all | solution.py:159
  98.0 0.0 copy-start.11
  98.1 1.9 %collective-permute-done.13 = bf16[1024,256]{1,0:T(8,128)(2,1)} collective-permute-done((bf16[1024,256]{1,0:T(8,128)(2,1)}, bf16[1024,256]{1,0:T(8,128)(2,1)}, u32[]{:S(2)}, u32[]{:S(2)}) %collective-permute-start.13) | collective-permute-done | bytes 524320 | tf_op jit(solution)/shard_map/ppermute | solution.py:153
  99.9 1.8 %fusion.16 = f32[256,512]{1,0:T(8,128)S(1)} fusion(bf16[1024,256]{1,0:T(8,128)(2,1)} %collective-permute-done.13, bf16[2048,512]{1,0:T(8,128)(2,1)} %param.10), kind=kOutput, calls=%fused_computation.31 | convolution fusion | flops 268435456 | bytes 2097152 | tf_op jit(solution)/shard_map/dot_general | solution.py:212
  101.8 1.5 fusion.8
  103.3 0.1 pad_maximum_fusion.1
  103.3 1.2 copy.25
  104.5 5.2 %all-to-all-done.1 = bf16[32,16,512]{2,1,0:T(8,128)(2,1)S(1)} async-done(((bf16[32,16,512]{2,1,0:T(8,128)(2,1)}), bf16[32,16,512]{2,1,0:T(8,128)(2,1)S(1)}, u32[]{:S(2)}, u32[]{:S(2)}) %all-to-all-start.1) | async-done | bytes 524320 | tf_op jit(solution)/shard_map/all_to_all | solution.py:159
  109.7 3.7 %all-to-all-start.2 = ((bf16[32,16,768]{2,1,0:T(8,128)(2,1)}), bf16[32,16,768]{2,1,0:T(8,128)(2,1)S(1)}, u32[]{:S(2)}, u32[]{:S(2)}) async-start(bf16[32,16,768]{2,1,0:T(8,128)(2,1)} %bitcast.13), calls=%async_computation.2 | async-start | bytes 1572864 | tf_op jit(solution)/shard_map/all_to_all | solution.py:159
  113.4 0.1 convert_reduce_fusion.1
  113.6 0.1 convert_reduce_fusion.2
  113.8 13.8 %all-to-all-done.2 = bf16[32,16,768]{2,1,0:T(8,128)(2,1)S(1)} async-done(((bf16[32,16,768]{2,1,0:T(8,128)(2,1)}), bf16[32,16,768]{2,1,0:T(8,128)(2,1)S(1)}, u32[]{:S(2)}, u32[]{:S(2)}) %all-to-all-start.2) | async-done | bytes 786464 | tf_op jit(solution)/shard_map/all_to_all | solution.py:159
  127.5 0.1 convert_reduce_fusion
  127.7 0.4 concatenate.16
  128.1 0.1 dynamic-slice_multiply_fusion
  128.3 10.9 %all_to_all.25 = f32[32,2,8]{2,1,0:T(2,128)S(1)} all-to-all(f32[32,2,8]{2,1,0:T(2,128)S(1)} %broadcast_in_dim.4), channel_id=1, replica_groups=mesh['dp_0'=4,'dp_1'=4,'dp_2'=2,'tensor'=8] {'dp_0','dp_1','dp_2'}, dimensions={0} | all-to-all | bytes 4096 | tf_op jit(solution)/shard_map/all_to_all | solution.py:165
  139.2 0.6 broadcast_in_dim.5
  139.8 4.6 %all-to-all-start.4 = ((f32[8,2,8]{2,1,0:T(2,128)}), f32[8,2,8]{2,1,0:T(2,128)S(1)}, u32[]{:S(2)}, u32[]{:S(2)}) async-start(f32[8,2,8]{2,1,0:T(2,128)} %broadcast_in_dim.5), calls=%async_computation.4 | async-start | bytes 16384 | tf_op jit(solution)/shard_map/all_to_all | solution.py:165
  144.4 0.1 mul.31
  144.5 6.5 %all-to-all-done.4 = f32[8,2,8]{2,1,0:T(2,128)S(1)} async-done(((f32[8,2,8]{2,1,0:T(2,128)}), f32[8,2,8]{2,1,0:T(2,128)S(1)}, u32[]{:S(2)}, u32[]{:S(2)}) %all-to-all-start.4) | async-done | bytes 544 | tf_op jit(solution)/shard_map/all_to_all | solution.py:165
  151.0 0.6 sqrt_add_fusion
  151.6 0.1 broadcast_bitcast_fusion
  151.7 0.8 multiply_divide_fusion
  (50 shorter events, 0.4 us)
Async XLA Ops:
  0.6 1.6 %copy-start.5 = (s32[32,16]{0,1:T(8,128)S(1)}, s32[32,16]{0,1:T(8,128)}, u32[]{:S(2)}) copy-start(s32[32,16]{0,1:T(8,128)} %param.17) | copy-start | bytes 6148
  0.6 1.6 %copy-start.6 = (s32[32,16]{0,1:T(8,128)S(1)}, s32[32,16]{0,1:T(8,128)}, u32[]{:S(2)}) copy-start(s32[32,16]{0,1:T(8,128)} %param.16) | copy-start | bytes 6148
  0.7 1.8 %copy-start = (bf16[2048,256]{1,0:T(8,128)(2,1)S(1)}, bf16[2048,256]{1,0:T(8,128)(2,1)}, u32[]{:S(2)}) copy-start(bf16[2048,256]{1,0:T(8,128)(2,1)} %q_next_ref.3) | copy-start | bytes 3145732
  0.7 1.9 %copy-start.1 = (bf16[2048,256]{1,0:T(8,128)(2,1)S(1)}, bf16[2048,256]{1,0:T(8,128)(2,1)}, u32[]{:S(2)}) copy-start(bf16[2048,256]{1,0:T(8,128)(2,1)} %do_next_ref.3) | copy-start | bytes 3145732
  0.7 1.9 %copy-start.2 = (bf16[2048,2]{0,1:T(2,128)(2,1)S(1)}, bf16[2048,2]{0,1:T(2,128)(2,1)}, u32[]{:S(2)}) copy-start(bf16[2048,2]{0,1:T(2,128)(2,1)} %param.14) | copy-start | bytes 24580
  0.7 1.8 %copy-start.3 = (bf16[2048,2]{0,1:T(2,128)(2,1)S(1)}, bf16[2048,2]{0,1:T(2,128)(2,1)}, u32[]{:S(2)}) copy-start(bf16[2048,2]{0,1:T(2,128)(2,1)} %param.15) | copy-start | bytes 24580
  5.3 12.0 %copy-start.8 = (bf16[2048,512]{1,0:T(8,128)(2,1)S(1)}, bf16[2048,512]{1,0:T(8,128)(2,1)}, u32[]{:S(2)}) copy-start(bf16[2048,512]{1,0:T(8,128)(2,1)} %param.10) | copy-start | bytes 6291460
  5.3 17.0 %collective-permute-start.3 = (bf16[1024,256]{1,0:T(8,128)(2,1)S(1)}, bf16[1024,256]{1,0:T(8,128)(2,1)}, u32[]{:S(2)}, u32[]{:S(2)}) collective-permute-start(bf16[1024,256]{1,0:T(8,128)(2,1)S(1)} %attention_grads.3), channel_id=1, source_target_pairs={{0,7},{1,0},{2,1},{3,2},{4,3},{5,4},{6,5},{7,6},{8,15},{9,8},{10,9... | collective-permute-start | bytes 1572872 | tf_op jit(solution)/shard_map/ppermute | solution.py:153
  11.8 14.1 %collective-permute-start.1 = (bf16[1024,256]{1,0:T(8,128)(2,1)S(1)}, bf16[1024,256]{1,0:T(8,128)(2,1)}, u32[]{:S(2)}, u32[]{:S(2)}) collective-permute-start(bf16[1024,256]{1,0:T(8,128)(2,1)S(1)} %attention_grads.3), channel_id=1, source_target_pairs={{0,1},{1,2},{2,3},{3,4},{4,5},{5,6},{6,7},{7,0},{8,9},{9,10},{10,1... | collective-permute-start | bytes 1572872 | tf_op jit(solution)/shard_map/ppermute | solution.py:153
  14.5 25.3 %collective-permute-start.2 = (bf16[1024,256]{1,0:T(8,128)(2,1)S(1)}, bf16[1024,256]{1,0:T(8,128)(2,1)S(1)}, u32[]{:S(2)}, u32[]{:S(2)}) collective-permute-start(bf16[1024,256]{1,0:T(8,128)(2,1)S(1)} %attention_grads.2), channel_id=1, source_target_pairs={{0,7},{1,0},{2,1},{3,2},{4,3},{5,4},{6,5},{7,6},{8,15},{9,8},{10,9... | collective-permute-start | bytes 1572872 | tf_op jit(solution)/shard_map/ppermute | solution.py:153
  17.3 19.5 %collective-permute-start = (bf16[1024,256]{1,0:T(8,128)(2,1)S(1)}, bf16[1024,256]{1,0:T(8,128)(2,1)}, u32[]{:S(2)}, u32[]{:S(2)}) collective-permute-start(bf16[1024,256]{1,0:T(8,128)(2,1)S(1)} %attention_grads.2), channel_id=1, source_target_pairs={{0,1},{1,2},{2,3},{3,4},{4,5},{5,6},{6,7},{7,0},{8,9},{9,10},{10,1... | collective-permute-start | bytes 1572872 | tf_op jit(solution)/shard_map/ppermute | solution.py:153
  22.3 32.7 %collective-permute-start.7 = (bf16[1024,256]{1,0:T(8,128)(2,1)}, bf16[1024,256]{1,0:T(8,128)(2,1)}, u32[]{:S(2)}, u32[]{:S(2)}) collective-permute-start(bf16[1024,256]{1,0:T(8,128)(2,1)} %collective-permute-done.3), channel_id=1, source_target_pairs={{0,7},{1,0},{2,1},{3,2},{4,3},{5,4},{6,5},{7,6},{8,15},{9,8},{10,9... | collective-permute-start | bytes 1572872 | tf_op jit(solution)/shard_map/ppermute | solution.py:153
  25.9 29.3 %collective-permute-start.5 = (bf16[1024,256]{1,0:T(8,128)(2,1)}, bf16[1024,256]{1,0:T(8,128)(2,1)}, u32[]{:S(2)}, u32[]{:S(2)}) collective-permute-start(bf16[1024,256]{1,0:T(8,128)(2,1)} %collective-permute-done.1), channel_id=1, source_target_pairs={{0,1},{1,2},{2,3},{3,4},{4,5},{5,6},{6,7},{7,0},{8,9},{9,10},{10,1... | collective-permute-start | bytes 1572872 | tf_op jit(solution)/shard_map/ppermute | solution.py:153
  36.8 22.5 %collective-permute-start.4 = (bf16[1024,256]{1,0:T(8,128)(2,1)}, bf16[1024,256]{1,0:T(8,128)(2,1)}, u32[]{:S(2)}, u32[]{:S(2)}) collective-permute-start(bf16[1024,256]{1,0:T(8,128)(2,1)} %collective-permute-done), channel_id=1, source_target_pairs={{0,1},{1,2},{2,3},{3,4},{4,5},{5,6},{6,7},{7,0},{8,9},{9,10},{10,1... | collective-permute-start | bytes 1572872 | tf_op jit(solution)/shard_map/ppermute | solution.py:153
  40.3 16.2 %copy-start.9 = (bf16[2048,512]{1,0:T(8,128)(2,1)S(1)}, bf16[2048,512]{1,0:T(8,128)(2,1)}, u32[]{:S(2)}) copy-start(bf16[2048,512]{1,0:T(8,128)(2,1)} %param.10) | copy-start | bytes 6291460
  41.5 47.6 %all-to-all-start = ((bf16[32,16,768]{2,1,0:T(8,128)(2,1)}), bf16[32,16,768]{2,1,0:T(8,128)(2,1)S(1)}, u32[]{:S(2)}, u32[]{:S(2)}) async-start(bf16[32,16,768]{2,1,0:T(8,128)(2,1)} %bitcast.6), calls=%async_computation | async-start | bytes 1572864 | tf_op jit(solution)/shard_map/all_to_all | solution.py:159
  52.0 14.1 %collective-permute-start.6 = (bf16[1024,256]{1,0:T(8,128)(2,1)S(1)}, bf16[1024,256]{1,0:T(8,128)(2,1)S(1)}, u32[]{:S(2)}, u32[]{:S(2)}) collective-permute-start(bf16[1024,256]{1,0:T(8,128)(2,1)S(1)} %collective-permute-done.2), channel_id=1, source_target_pairs={{0,7},{1,0},{2,1},{3,2},{4,3},{5,4},{6,5},{7,6},{8,15},{9,8},{10,9... | collective-permute-start | bytes 1572872 | tf_op jit(solution)/shard_map/ppermute | solution.py:153
  55.0 22.4 %collective-permute-start.11 = (bf16[1024,256]{1,0:T(8,128)(2,1)}, bf16[1024,256]{1,0:T(8,128)(2,1)}, u32[]{:S(2)}, u32[]{:S(2)}) collective-permute-start(bf16[1024,256]{1,0:T(8,128)(2,1)} %collective-permute-done.7), channel_id=1, source_target_pairs={{0,7},{1,0},{2,1},{3,2},{4,3},{5,4},{6,5},{7,6},{8,15},{9,8},{10,9... | collective-permute-start | bytes 1572872 | tf_op jit(solution)/shard_map/ppermute | solution.py:153
  55.1 26.9 %collective-permute-start.9 = (bf16[1024,256]{1,0:T(8,128)(2,1)}, bf16[1024,256]{1,0:T(8,128)(2,1)}, u32[]{:S(2)}, u32[]{:S(2)}) collective-permute-start(bf16[1024,256]{1,0:T(8,128)(2,1)} %collective-permute-done.5), channel_id=1, source_target_pairs={{0,1},{1,2},{2,3},{3,4},{4,5},{5,6},{6,7},{7,0},{8,9},{9,10},{10,1... | collective-permute-start | bytes 1572872 | tf_op jit(solution)/shard_map/ppermute | solution.py:153
  59.2 22.8 %collective-permute-start.8 = (bf16[1024,256]{1,0:T(8,128)(2,1)}, bf16[1024,256]{1,0:T(8,128)(2,1)}, u32[]{:S(2)}, u32[]{:S(2)}) collective-permute-start(bf16[1024,256]{1,0:T(8,128)(2,1)} %collective-permute-done.4), channel_id=1, source_target_pairs={{0,1},{1,2},{2,3},{3,4},{4,5},{5,6},{6,7},{7,0},{8,9},{9,10},{10,1... | collective-permute-start | bytes 1572872 | tf_op jit(solution)/shard_map/ppermute | solution.py:153
  66.1 0.8 copy-start.12
  68.4 15.2 %copy-start.10 = (bf16[2048,512]{1,0:T(8,128)(2,1)S(1)}, bf16[2048,512]{1,0:T(8,128)(2,1)}, u32[]{:S(2)}) copy-start(bf16[2048,512]{1,0:T(8,128)(2,1)} %param.10) | copy-start | bytes 6291460
  68.4 20.2 %collective-permute-start.10 = (bf16[1024,256]{1,0:T(8,128)(2,1)}, bf16[1024,256]{1,0:T(8,128)(2,1)S(1)}, u32[]{:S(2)}, u32[]{:S(2)}) collective-permute-start(bf16[1024,256]{1,0:T(8,128)(2,1)} %copy-done.12), channel_id=1, source_target_pairs={{0,7},{1,0},{2,1},{3,2},{4,3},{5,4},{6,5},{7,6},{8,15},{9,8},{10,9... | collective-permute-start | bytes 1572872 | tf_op jit(solution)/shard_map/ppermute | solution.py:153
  77.4 22.5 %collective-permute-start.13 = (bf16[1024,256]{1,0:T(8,128)(2,1)}, bf16[1024,256]{1,0:T(8,128)(2,1)}, u32[]{:S(2)}, u32[]{:S(2)}) collective-permute-start(bf16[1024,256]{1,0:T(8,128)(2,1)} %collective-permute-done.11), channel_id=1, source_target_pairs={{0,7},{1,0},{2,1},{3,2},{4,3},{5,4},{6,5},{7,6},{8,15},{9,8},{10,9... | collective-permute-start | bytes 1572872 | tf_op jit(solution)/shard_map/ppermute | solution.py:153
  82.1 19.7 %collective-permute-start.12 = (bf16[1024,256]{1,0:T(8,128)(2,1)}, bf16[1024,256]{1,0:T(8,128)(2,1)}, u32[]{:S(2)}, u32[]{:S(2)}) collective-permute-start(bf16[1024,256]{1,0:T(8,128)(2,1)} %collective-permute-done.8), channel_id=1, source_target_pairs={{0,1},{1,2},{2,3},{3,4},{4,5},{5,6},{6,7},{7,0},{8,9},{9,10},{10,1... | collective-permute-start | bytes 1572872 | tf_op jit(solution)/shard_map/ppermute | solution.py:153
  89.2 20.5 %all-to-all-start.1 = ((bf16[32,16,512]{2,1,0:T(8,128)(2,1)}), bf16[32,16,512]{2,1,0:T(8,128)(2,1)S(1)}, u32[]{:S(2)}, u32[]{:S(2)}) async-start(bf16[32,16,512]{2,1,0:T(8,128)(2,1)} %bitcast.9), calls=%async_computation.1 | async-start | bytes 1048576 | tf_op jit(solution)/shard_map/all_to_all | solution.py:159
  98.0 3.7 %copy-start.11 = (bf16[2048,512]{1,0:T(8,128)(2,1)S(1)}, bf16[2048,512]{1,0:T(8,128)(2,1)}, u32[]{:S(2)}) copy-start(bf16[2048,512]{1,0:T(8,128)(2,1)} %param.10) | copy-start | bytes 6291460
  109.7 17.9 %all-to-all-start.2 = ((bf16[32,16,768]{2,1,0:T(8,128)(2,1)}), bf16[32,16,768]{2,1,0:T(8,128)(2,1)S(1)}, u32[]{:S(2)}, u32[]{:S(2)}) async-start(bf16[32,16,768]{2,1,0:T(8,128)(2,1)} %bitcast.13), calls=%async_computation.2 | async-start | bytes 1572864 | tf_op jit(solution)/shard_map/all_to_all | solution.py:159
  113.4 37.6 %copy-start.7 = (f32[2,8]{1,0:T(2,128)S(1)}, f32[2,8]{1,0:T(2,128)}, u32[]{:S(2)}) copy-start(f32[2,8]{1,0:T(2,128)} %param.19) | copy-start | bytes 196
  113.4 38.3 %copy-start.4 = (f32[16,2,1024]{2,1,0:T(2,128)S(1)}, f32[16,2,1024]{2,1,0:T(2,128)}, u32[]{:S(2)}) copy-start(f32[16,2,1024]{2,1,0:T(2,128)} %param.18) | copy-start | bytes 393220
  139.8 11.2 %all-to-all-start.4 = ((f32[8,2,8]{2,1,0:T(2,128)}), f32[8,2,8]{2,1,0:T(2,128)S(1)}, u32[]{:S(2)}, u32[]{:S(2)}) async-start(f32[8,2,8]{2,1,0:T(2,128)} %broadcast_in_dim.5), calls=%async_computation.4 | async-start | bytes 16384 | tf_op jit(solution)/shard_map/all_to_all | solution.py:165

commit v2 on v1

--- a/solution.py
+++ b/solution.py
@@ -149,6 +149,44 @@
     )(fill, cont, queries, queries, out_grads, out_grads, keys_values, lse, lse, delta, delta)
 
 
+def product_kernel(turned_ref, *refs):
+    *halves, out_ref = refs
+    half = halves[0].shape[0]
+    width = halves[0].shape[1]
+    rows = turned_ref.shape[0]
+    chunk = 256
+    for i in range(len(halves) // 2):
+        for r in range(0, rows, chunk):
+            total = lax.dot_general(
+                turned_ref[r : r + chunk, 0:half],
+                halves[2 * i][...],
+                NN,
+                preferred_element_type=jnp.float32,
+            ) + lax.dot_general(
+                turned_ref[r : r + chunk, half : 2 * half],
+                halves[2 * i + 1][...],
+                NN,
+                preferred_element_type=jnp.float32,
+            )
+            out_ref[r : r + chunk, i * width : (i + 1) * width] = total.astype(jnp.bfloat16)
+
+
+def product(turned, pairs):
+    halves = sum([list(pair) for pair in pairs], [])
+    vmem = pl.BlockSpec(memory_space=pltpu.VMEM)
+    return pl.pallas_call(
+        product_kernel,
+        in_specs=[vmem] * (1 + len(halves)),
+        out_specs=vmem,
+        out_shape=jax.ShapeDtypeStruct(
+            (turned.shape[0], len(pairs) * halves[0].shape[1]), jnp.bfloat16
+        ),
+        compiler_params=pltpu.CompilerParams(vmem_limit_bytes=32 * 1024 * 1024),
+        cost_estimate=pl.CostEstimate(flops=1000, bytes_accessed=1000, transcendentals=0),
+        name="projection_product",
+    )(turned, *halves)
+
+
 def shifted(array, steps, length):
     return lax.ppermute(array, "tensor", [(i, (i + steps) % length) for i in range(length)])
 
@@ -194,7 +232,7 @@
         attention(first, half, 4, fill, cont, queries, out_grads, kv, log_sums.T, deltas.T)
         for first in (0, half)
     ]
-    inputs = [layer_input[: half * BLK], layer_input[half * BLK :]]
+    turned = layer_input.T
 
     blocks = {0: list(halves)}
     right, left = list(halves), list(halves)
@@ -207,17 +245,9 @@
         blocks[step] = list(left)
     blocks[far] = [shifted(right[0], 1, ring), shifted(left[1], -1, ring)]
 
-    def product(offset):
-        one, two = (
-            lax.dot_general(x, b, TN, preferred_element_type=jnp.float32)
-            for x, b in zip(inputs, blocks[offset])
-        )
-        return (one + two).astype(jnp.bfloat16)
-
     summed = {}
     for offsets in ((0, -1, 1), (-2, 2), (-3, 3, far)):
-        together = jnp.concatenate([product(o) for o in offsets], 1)
-        total = sum_at_owner(together, DP)
+        total = sum_at_owner(product(turned, [blocks[o] for o in offsets]), DP)
         for i, o in enumerate(offsets):
             summed[o % ring] = total[:, i * 2 * HD : (i + 1) * 2 * HD]
 

time: 153 us -> 156 us (1.020)
  matrix products: 19.1 us -> 0 us
  Pallas kernels: 5.52 us -> 19.3 us
  starting transfers between devices: 51.7 us -> 56.7 us
  waiting for transfers between devices: 54.7 us -> 58 us
    dot_general x16 -> x0, matrix products: 19.1 us -> none  [product(): lax.dot_general(x, b, TN, preferred_element_type=jnp.float32)]
    pallas_call x0 -> x3, Pallas kernels: none -> 12.3 us  [product(): pl.pallas_call(product_kernel, in_specs=[vmem] * (1 + len(halves)), out_s...]
    ppermute x14, waiting for transfers between devices: 29.3 us -> 38.8 us  [shifted(): lax.ppermute(array, 'tensor', [(i, (i + steps) % length) for i in range(l...]
    all_to_all x3, waiting for transfers between devices: 18.9 us -> 12.7 us  [sum_at_owner(): lax.all_to_all(parts, axes, split_axis=0, concat_axis=0, tiled=True)]
    all_to_all x3, starting transfers between devices: 23.1 us -> 26.7 us  [sum_at_owner(): lax.all_to_all(parts, axes, split_axis=0, concat_axis=0, tiled=True)]
    concatenate x3 -> x0, local copies, waits for them, and re-layouts: 3.34 us -> none  [per_device(): together = jnp.concatenate([product(o) for o in offsets], 1)]
    unnamed x29 -> x20, local copies, waits for them, and re-layouts: 2.56 us -> 4.64 us
  transfers between devices with their start and end apart: 18 -> 18, of which waited for: 11 -> 9; matrix products, arithmetic and copies ran while one was open for 15% -> 3% of each run, Pallas kernels for 2% -> 10%
where the time goes in v2:
time: 156 us; the launch traced here: 155 us
  waiting for transfers between devices  58 us (37%)
  starting transfers between devices  56.7 us (36%)
  Pallas kernels  19.3 us (12%)
  blocking collectives  10.9 us (7%)
  local copies, waits for them, and re-layouts  6.08 us (4%)
  other arithmetic  3.08 us (2%)
    ppermute x14, waiting for transfers between devices, shifted(): lax.ppermute(array, 'tensor', [(i, (i + steps) % length) for i in range(l...  38.8 us
    all_to_all x3, starting transfers between devices, sum_at_owner(): lax.all_to_all(parts, axes, split_axis=0, concat_axis=0, tiled=True)  26.7 us
    ppermute x14, starting transfers between devices, shifted(): lax.ppermute(array, 'tensor', [(i, (i + steps) % length) for i in range(l...  24.1 us
    all_to_all x3, waiting for transfers between devices, sum_at_owner(): lax.all_to_all(parts, axes, split_axis=0, concat_axis=0, tiled=True)  12.7 us
    pallas_call x3, Pallas kernels, product(): pl.pallas_call(product_kernel, in_specs=[vmem] * (1 + len(halves)), out_s...  12.3 us
    all_to_all x1, blocking collectives, taken_together(): lax.all_to_all(jnp.broadcast_to(array[None], (length, *array.shape)), axe...  10.9 us
    pallas_call x2, Pallas kernels, attention(): pl.pallas_call(functools.partial(attention_kernel, first, per_step, tile_...  6.97 us
    all_to_all x1, waiting for transfers between devices, taken_together(): lax.all_to_all(jnp.broadcast_to(array[None], (length, *array.shape)), axe...  6.5 us
  transfers between devices with their start and end apart: 18, of which 9 were waited for; matrix products, arithmetic and copies ran while one was open for 3% of the time, Pallas kernels for 10%

profile of v2, /device:TPU:1, one launch (start us, length us, event | category | flops | bytes accessed | tf_op | source)
XLA Modules:
  0.0 155.0 jit_solution(10021638370479060064)
XLA Ops:
  0.6 0.0 copy-start.5
  0.7 1.5 copy.28
  2.2 0.0 copy-done.5
  2.2 0.0 copy-done.6
  2.2 0.2 dynamic-slice_reduce_fusion
  2.4 0.0 copy-done
  2.4 0.1 copy-done.1
  2.5 0.0 copy-done.2
  2.5 3.5 %attention_grads.2.refs_0_ = bf16[1024,256]{1,0:T(8,128)(2,1)} custom-call(s32[16]{0:T(128)S(1)} %get-tuple-element.18.fill_ref, s32[16]{0:T(128)S(1)} %get-tuple-element.17.cont_ref, bf16[2048,256]{1,0:T(8,128)(2,1)S(1)} %copy-done, bf16[2048,256]{1,0:T(8,128)(2,1)S(1)} %copy-done, bf16[2048,256]{1,0:T(8,128)(2,1)S(1)} %copy-done.1, ...), custom_call_target="tpu_custom_call" | custom-call | flops 536870912 | bytes 2621440 | tf_op jit(solution)/shard_map/attention_grads/pallas_call | solution.py:123
  6.0 2.5 %collective-permute-start = (bf16[1024,256]{1,0:T(8,128)(2,1)}, bf16[1024,256]{1,0:T(8,128)(2,1)}, u32[]{:S(2)}, u32[]{:S(2)}) collective-permute-start(bf16[1024,256]{1,0:T(8,128)(2,1)} %attention_grads.2.refs_0_), channel_id=1, source_target_pairs={{0,1},{1,2},{2,3},{3,4},{4,5},{5,6},{6,7},{7,0},{8,9},{9,10},{10,1... | collective-permute-start | bytes 1572872 | tf_op jit(solution)/shard_map/ppermute | solution.py:191
  8.5 3.5 %attention_grads.3.refs_1_ = bf16[1024,256]{1,0:T(8,128)(2,1)} custom-call(s32[16]{0:T(128)S(1)} %get-tuple-element.18.fill_ref, s32[16]{0:T(128)S(1)} %get-tuple-element.17.cont_ref, bf16[2048,256]{1,0:T(8,128)(2,1)S(1)} %copy-done, bf16[2048,256]{1,0:T(8,128)(2,1)S(1)} %copy-done, bf16[2048,256]{1,0:T(8,128)(2,1)S(1)} %copy-done.1, ...), custom_call_target="tpu_custom_call" | custom-call | flops 536870912 | bytes 2621440 | tf_op jit(solution)/shard_map/attention_grads/pallas_call | solution.py:123
  12.0 3.9 %collective-permute-start.3 = (bf16[1024,256]{1,0:T(8,128)(2,1)}, bf16[1024,256]{1,0:T(8,128)(2,1)}, u32[]{:S(2)}, u32[]{:S(2)}) collective-permute-start(bf16[1024,256]{1,0:T(8,128)(2,1)} %attention_grads.3.refs_1_), channel_id=1, source_target_pairs={{0,7},{1,0},{2,1},{3,2},{4,3},{5,4},{6,5},{7,6},{8,15},{9,8},{10,9... | collective-permute-start | bytes 1572872 | tf_op jit(solution)/shard_map/ppermute | solution.py:191
  15.9 0.0 collective-permute-start.1
  15.9 2.7 %collective-permute-start.2 = (bf16[1024,256]{1,0:T(8,128)(2,1)}, bf16[1024,256]{1,0:T(8,128)(2,1)}, u32[]{:S(2)}, u32[]{:S(2)}) collective-permute-start(bf16[1024,256]{1,0:T(8,128)(2,1)} %attention_grads.2.refs_0_), channel_id=1, source_target_pairs={{0,7},{1,0},{2,1},{3,2},{4,3},{5,4},{6,5},{7,6},{8,15},{9,8},{10,9... | collective-permute-start | bytes 1572872 | tf_op jit(solution)/shard_map/ppermute | solution.py:191
  18.6 5.8 %collective-permute-done.refs_2_ = bf16[1024,256]{1,0:T(8,128)(2,1)} collective-permute-done((bf16[1024,256]{1,0:T(8,128)(2,1)}, bf16[1024,256]{1,0:T(8,128)(2,1)}, u32[]{:S(2)}, u32[]{:S(2)}) %collective-permute-start) | collective-permute-done | bytes 524320 | tf_op jit(solution)/shard_map/ppermute | solution.py:191
  24.3 0.0 collective-permute-start.4
  24.3 2.4 %collective-permute-done.3.refs_5_ = bf16[1024,256]{1,0:T(8,128)(2,1)} collective-permute-done((bf16[1024,256]{1,0:T(8,128)(2,1)}, bf16[1024,256]{1,0:T(8,128)(2,1)}, u32[]{:S(2)}, u32[]{:S(2)}) %collective-permute-start.3) | collective-permute-done | bytes 524320 | tf_op jit(solution)/shard_map/ppermute | solution.py:191
  26.8 3.4 %collective-permute-start.7 = (bf16[1024,256]{1,0:T(8,128)(2,1)}, bf16[1024,256]{1,0:T(8,128)(2,1)S(1)}, u32[]{:S(2)}, u32[]{:S(2)}) collective-permute-start(bf16[1024,256]{1,0:T(8,128)(2,1)} %collective-permute-done.3.refs_5_), channel_id=1, source_target_pairs={{0,7},{1,0},{2,1},{3,2},{4,3},{5,4},{6,5},{7,6},{8,15},{9,8},{10,9... | collective-permute-start | bytes 1572872 | tf_op jit(solution)/shard_map/ppermute | solution.py:191
  30.2 2.9 %copy.19 = bf16[2048,512]{0,1:T(8,128)(2,1)S(1)} copy(bf16[2048,512]{1,0:T(8,128)(2,1)} %param.10) | data formatting | bytes 4194304 | tf_op args[0]
  33.1 2.4 %collective-permute-done.1.refs_3_ = bf16[1024,256]{1,0:T(8,128)(2,1)} collective-permute-done((bf16[1024,256]{1,0:T(8,128)(2,1)}, bf16[1024,256]{1,0:T(8,128)(2,1)}, u32[]{:S(2)}, u32[]{:S(2)}) %collective-permute-start.1) | collective-permute-done | bytes 524320 | tf_op jit(solution)/shard_map/ppermute | solution.py:191
  35.6 2.4 %collective-permute-done.2.refs_4_ = bf16[1024,256]{1,0:T(8,128)(2,1)} collective-permute-done((bf16[1024,256]{1,0:T(8,128)(2,1)}, bf16[1024,256]{1,0:T(8,128)(2,1)}, u32[]{:S(2)}, u32[]{:S(2)}) %collective-permute-start.2) | collective-permute-done | bytes 524320 | tf_op jit(solution)/shard_map/ppermute | solution.py:191
  38.0 4.5 %projection_product.3 = bf16[512,768]{1,0:T(8,128)(2,1)} custom-call(bf16[512,2048]{1,0:T(8,128)(2,1)S(1)} %bitcast.16, bf16[1024,256]{1,0:T(8,128)(2,1)} %attention_grads.2.refs_0_, bf16[1024,256]{1,0:T(8,128)(2,1)} %attention_grads.3.refs_1_, bf16[1024,256]{1,0:T(8,128)(2,1)} %collective-permute-done.refs_2_, ...), custom_call_target="tpu_custom_call" | custom-call | flops 1000 | bytes 1000 | tf_op jit(solution)/shard_map/projection_product/pallas_call | solution.py:177
  42.6 9.9 %all-to-all-start = ((bf16[32,16,768]{2,1,0:T(8,128)(2,1)}), bf16[32,16,768]{2,1,0:T(8,128)(2,1)}, u32[]{:S(2)}, u32[]{:S(2)}) async-start(bf16[32,16,768]{2,1,0:T(8,128)(2,1)} %bitcast.4), calls=%async_computation | async-start | bytes 1572864 | tf_op jit(solution)/shard_map/all_to_all | solution.py:197
  52.4 0.3 collective-permute-start.5
  52.7 3.3 %collective-permute-start.6 = (bf16[1024,256]{1,0:T(8,128)(2,1)}, bf16[1024,256]{1,0:T(8,128)(2,1)}, u32[]{:S(2)}, u32[]{:S(2)}) collective-permute-start(bf16[1024,256]{1,0:T(8,128)(2,1)} %collective-permute-done.2.refs_4_), channel_id=1, source_target_pairs={{0,7},{1,0},{2,1},{3,2},{4,3},{5,4},{6,5},{7,6},{8,15},{9,8},{10,9... | collective-permute-start | bytes 1572872 | tf_op jit(solution)/shard_map/ppermute | solution.py:191
  56.0 0.0 collective-permute-done.4.refs_0_
  56.0 0.0 collective-permute-start.8
  56.0 0.0 collective-permute-done.7.refs_3_
  56.0 2.7 %collective-permute-start.11 = (bf16[1024,256]{1,0:T(8,128)(2,1)S(1)}, bf16[1024,256]{1,0:T(8,128)(2,1)}, u32[]{:S(2)}, u32[]{:S(2)}) collective-permute-start(bf16[1024,256]{1,0:T(8,128)(2,1)S(1)} %collective-permute-done.7.refs_3_), channel_id=1, source_target_pairs={{0,7},{1,0},{2,1},{3,2},{4,3},{5,4},{6,5},{7,6},{8,15},{9,8},{10,9... | collective-permute-start | bytes 1572872 | tf_op jit(solution)/shard_map/ppermute | solution.py:191
  58.7 9.6 %collective-permute-done.5.refs_1_ = bf16[1024,256]{1,0:T(8,128)(2,1)} collective-permute-done((bf16[1024,256]{1,0:T(8,128)(2,1)}, bf16[1024,256]{1,0:T(8,128)(2,1)}, u32[]{:S(2)}, u32[]{:S(2)}) %collective-permute-start.5) | collective-permute-done | bytes 524320 | tf_op jit(solution)/shard_map/ppermute | solution.py:191
  68.3 0.0 collective-permute-start.9
  68.3 0.0 collective-permute-done.6.refs_2_
  68.3 2.7 %collective-permute-start.10 = (bf16[1024,256]{1,0:T(8,128)(2,1)}, bf16[1024,256]{1,0:T(8,128)(2,1)}, u32[]{:S(2)}, u32[]{:S(2)}) collective-permute-start(bf16[1024,256]{1,0:T(8,128)(2,1)} %collective-permute-done.6.refs_2_), channel_id=1, source_target_pairs={{0,7},{1,0},{2,1},{3,2},{4,3},{5,4},{6,5},{7,6},{8,15},{9,8},{10,9... | collective-permute-start | bytes 1572872 | tf_op jit(solution)/shard_map/ppermute | solution.py:191
  71.0 8.6 %collective-permute-done.8.refs_0_ = bf16[1024,256]{1,0:T(8,128)(2,1)} collective-permute-done((bf16[1024,256]{1,0:T(8,128)(2,1)S(1)}, bf16[1024,256]{1,0:T(8,128)(2,1)}, u32[]{:S(2)}, u32[]{:S(2)}) %collective-permute-start.8) | collective-permute-done | bytes 524320 | tf_op jit(solution)/shard_map/ppermute | solution.py:191
  79.6 0.0 collective-permute-start.12
  79.6 0.0 collective-permute-done.11.refs_3_
  79.6 2.7 %collective-permute-start.13 = (bf16[1024,256]{1,0:T(8,128)(2,1)}, bf16[1024,256]{1,0:T(8,128)(2,1)}, u32[]{:S(2)}, u32[]{:S(2)}) collective-permute-start(bf16[1024,256]{1,0:T(8,128)(2,1)} %collective-permute-done.11.refs_3_), channel_id=1, source_target_pairs={{0,7},{1,0},{2,1},{3,2},{4,3},{5,4},{6,5},{7,6},{8,15},{9,8},{10,9... | collective-permute-start | bytes 1572872 | tf_op jit(solution)/shard_map/ppermute | solution.py:191
  82.2 3.3 %projection_product.4 = bf16[512,512]{1,0:T(8,128)(2,1)} custom-call(bf16[512,2048]{1,0:T(8,128)(2,1)S(1)} %bitcast.17, bf16[1024,256]{1,0:T(8,128)(2,1)S(1)} %collective-permute-done.4.refs_0_, bf16[1024,256]{1,0:T(8,128)(2,1)} %collective-permute-done.5.refs_1_, bf16[1024,256]{1,0:T(8,128)(2,1)} %collective-permute-done.6.refs_2_, ...), custom_call_target="tpu_custom_call" | custom-call | flops 1000 | bytes 1000 | tf_op jit(solution)/shard_map/projection_product/pallas_call | solution.py:177
  85.5 0.0 all-to-all-done
  85.5 9.0 %all-to-all-start.1 = ((bf16[32,16,512]{2,1,0:T(8,128)(2,1)}), bf16[32,16,512]{2,1,0:T(8,128)(2,1)S(1)}, u32[]{:S(2)}, u32[]{:S(2)}) async-start(bf16[32,16,512]{2,1,0:T(8,128)(2,1)} %bitcast.5), calls=%async_computation.1 | async-start | bytes 1048576 | tf_op jit(solution)/shard_map/all_to_all | solution.py:197
  94.5 0.0 collective-permute-done.9.refs_1_
  94.5 0.0 collective-permute-done.10.refs_2_
  94.5 7.5 %collective-permute-done.12.refs_4_ = bf16[1024,256]{1,0:T(8,128)(2,1)} collective-permute-done((bf16[1024,256]{1,0:T(8,128)(2,1)}, bf16[1024,256]{1,0:T(8,128)(2,1)}, u32[]{:S(2)}, u32[]{:S(2)}) %collective-permute-start.12) | collective-permute-done | bytes 524320 | tf_op jit(solution)/shard_map/ppermute | solution.py:191
  102.0 0.0 collective-permute-done.13.refs_5_
  102.0 4.5 %projection_product.5 = bf16[512,768]{1,0:T(8,128)(2,1)} custom-call(bf16[512,2048]{1,0:T(8,128)(2,1)S(1)} %bitcast.18, bf16[1024,256]{1,0:T(8,128)(2,1)} %collective-permute-done.8.refs_0_, bf16[1024,256]{1,0:T(8,128)(2,1)} %collective-permute-done.9.refs_1_, bf16[1024,256]{1,0:T(8,128)(2,1)} %collective-permute-done.10.refs_2_, ...), custom_call_target="tpu_custom_call" | custom-call | flops 1000 | bytes 1000 | tf_op jit(solution)/shard_map/projection_product/pallas_call | solution.py:177
  106.6 0.0 all-to-all-done.1
  106.6 7.8 %all-to-all-start.2 = ((bf16[32,16,768]{2,1,0:T(8,128)(2,1)}), bf16[32,16,768]{2,1,0:T(8,128)(2,1)S(1)}, u32[]{:S(2)}, u32[]{:S(2)}) async-start(bf16[32,16,768]{2,1,0:T(8,128)(2,1)} %bitcast.6), calls=%async_computation.2 | async-start | bytes 1572864 | tf_op jit(solution)/shard_map/all_to_all | solution.py:197
  114.4 0.0 copy-start.7
  114.4 0.0 copy-start.4
  114.4 1.3 convert_reduce_fusion.1
  115.8 0.1 convert_reduce_fusion.2
  116.0 12.6 %all-to-all-done.2 = bf16[32,16,768]{2,1,0:T(8,128)(2,1)S(1)} async-done(((bf16[32,16,768]{2,1,0:T(8,128)(2,1)}), bf16[32,16,768]{2,1,0:T(8,128)(2,1)S(1)}, u32[]{:S(2)}, u32[]{:S(2)}) %all-to-all-start.2) | async-done | bytes 786464 | tf_op jit(solution)/shard_map/all_to_all | solution.py:197
  128.6 0.1 convert_reduce_fusion
  128.8 0.4 concatenate.4
  129.2 0.1 dynamic-slice_multiply_fusion
  129.4 10.9 %all_to_all.25 = f32[32,2,8]{2,1,0:T(2,128)S(1)} all-to-all(f32[32,2,8]{2,1,0:T(2,128)S(1)} %broadcast_in_dim.4), channel_id=1, replica_groups=mesh['dp_0'=4,'dp_1'=4,'dp_2'=2,'tensor'=8] {'dp_0','dp_1','dp_2'}, dimensions={0} | all-to-all | bytes 4096 | tf_op jit(solution)/shard_map/all_to_all | solution.py:203
  140.3 0.6 broadcast_in_dim.5
  140.9 6.0 %all-to-all-start.4 = ((f32[8,2,8]{2,1,0:T(2,128)}), f32[8,2,8]{2,1,0:T(2,128)S(1)}, u32[]{:S(2)}, u32[]{:S(2)}) async-start(f32[8,2,8]{2,1,0:T(2,128)} %broadcast_in_dim.5), calls=%async_computation.4 | async-start | bytes 16384 | tf_op jit(solution)/shard_map/all_to_all | solution.py:203
  146.9 0.1 mul.31
  147.0 6.5 %all-to-all-done.4 = f32[8,2,8]{2,1,0:T(2,128)S(1)} async-done(((f32[8,2,8]{2,1,0:T(2,128)}), f32[8,2,8]{2,1,0:T(2,128)S(1)}, u32[]{:S(2)}, u32[]{:S(2)}) %all-to-all-start.4) | async-done | bytes 544 | tf_op jit(solution)/shard_map/all_to_all | solution.py:203
  153.5 0.6 sqrt_add_fusion
  154.0 0.1 broadcast_bitcast_fusion
  154.1 0.0 copy-done.4
  154.1 0.8 multiply_divide_fusion
  (22 shorter events, 0.3 us)
Async XLA Ops:
  0.6 1.6 %copy-start.5 = (s32[32,16]{0,1:T(8,128)S(1)}, s32[32,16]{0,1:T(8,128)}, u32[]{:S(2)}) copy-start(s32[32,16]{0,1:T(8,128)} %param.17) | copy-start | bytes 6148
  0.6 1.6 %copy-start.6 = (s32[32,16]{0,1:T(8,128)S(1)}, s32[32,16]{0,1:T(8,128)}, u32[]{:S(2)}) copy-start(s32[32,16]{0,1:T(8,128)} %param.16) | copy-start | bytes 6148
  0.7 1.8 %copy-start = (bf16[2048,256]{1,0:T(8,128)(2,1)S(1)}, bf16[2048,256]{1,0:T(8,128)(2,1)}, u32[]{:S(2)}) copy-start(bf16[2048,256]{1,0:T(8,128)(2,1)} %q_next_ref.3) | copy-start | bytes 3145732
  0.7 1.9 %copy-start.1 = (bf16[2048,256]{1,0:T(8,128)(2,1)S(1)}, bf16[2048,256]{1,0:T(8,128)(2,1)}, u32[]{:S(2)}) copy-start(bf16[2048,256]{1,0:T(8,128)(2,1)} %do_next_ref.3) | copy-start | bytes 3145732
  0.7 1.9 %copy-start.2 = (bf16[2048,2]{0,1:T(2,128)(2,1)S(1)}, bf16[2048,2]{0,1:T(2,128)(2,1)}, u32[]{:S(2)}) copy-start(bf16[2048,2]{0,1:T(2,128)(2,1)} %param.14) | copy-start | bytes 24580
  0.7 1.8 %copy-start.3 = (bf16[2048,2]{0,1:T(2,128)(2,1)S(1)}, bf16[2048,2]{0,1:T(2,128)(2,1)}, u32[]{:S(2)}) copy-start(bf16[2048,2]{0,1:T(2,128)(2,1)} %param.15) | copy-start | bytes 24580
  6.0 18.4 %collective-permute-start = (bf16[1024,256]{1,0:T(8,128)(2,1)}, bf16[1024,256]{1,0:T(8,128)(2,1)}, u32[]{:S(2)}, u32[]{:S(2)}) collective-permute-start(bf16[1024,256]{1,0:T(8,128)(2,1)} %attention_grads.2.refs_0_), channel_id=1, source_target_pairs={{0,1},{1,2},{2,3},{3,4},{4,5},{5,6},{6,7},{7,0},{8,9},{9,10},{10,1... | collective-permute-start | bytes 1572872 | tf_op jit(solution)/shard_map/ppermute | solution.py:191
  12.0 14.8 %collective-permute-start.3 = (bf16[1024,256]{1,0:T(8,128)(2,1)}, bf16[1024,256]{1,0:T(8,128)(2,1)}, u32[]{:S(2)}, u32[]{:S(2)}) collective-permute-start(bf16[1024,256]{1,0:T(8,128)(2,1)} %attention_grads.3.refs_1_), channel_id=1, source_target_pairs={{0,7},{1,0},{2,1},{3,2},{4,3},{5,4},{6,5},{7,6},{8,15},{9,8},{10,9... | collective-permute-start | bytes 1572872 | tf_op jit(solution)/shard_map/ppermute | solution.py:191
  15.9 19.7 %collective-permute-start.1 = (bf16[1024,256]{1,0:T(8,128)(2,1)}, bf16[1024,256]{1,0:T(8,128)(2,1)}, u32[]{:S(2)}, u32[]{:S(2)}) collective-permute-start(bf16[1024,256]{1,0:T(8,128)(2,1)} %attention_grads.3.refs_1_), channel_id=1, source_target_pairs={{0,1},{1,2},{2,3},{3,4},{4,5},{5,6},{6,7},{7,0},{8,9},{9,10},{10,1... | collective-permute-start | bytes 1572872 | tf_op jit(solution)/shard_map/ppermute | solution.py:191
  15.9 22.1 %collective-permute-start.2 = (bf16[1024,256]{1,0:T(8,128)(2,1)}, bf16[1024,256]{1,0:T(8,128)(2,1)}, u32[]{:S(2)}, u32[]{:S(2)}) collective-permute-start(bf16[1024,256]{1,0:T(8,128)(2,1)} %attention_grads.2.refs_0_), channel_id=1, source_target_pairs={{0,7},{1,0},{2,1},{3,2},{4,3},{5,4},{6,5},{7,6},{8,15},{9,8},{10,9... | collective-permute-start | bytes 1572872 | tf_op jit(solution)/shard_map/ppermute | solution.py:191
  24.3 31.7 %collective-permute-start.4 = (bf16[1024,256]{1,0:T(8,128)(2,1)}, bf16[1024,256]{1,0:T(8,128)(2,1)S(1)}, u32[]{:S(2)}, u32[]{:S(2)}) collective-permute-start(bf16[1024,256]{1,0:T(8,128)(2,1)} %collective-permute-done.refs_2_), channel_id=1, source_target_pairs={{0,1},{1,2},{2,3},{3,4},{4,5},{5,6},{6,7},{7,0},{8,9},{9,10},{10,1... | collective-permute-start | bytes 1572872 | tf_op jit(solution)/shard_map/ppermute | solution.py:191
  26.8 29.2 %collective-permute-start.7 = (bf16[1024,256]{1,0:T(8,128)(2,1)}, bf16[1024,256]{1,0:T(8,128)(2,1)S(1)}, u32[]{:S(2)}, u32[]{:S(2)}) collective-permute-start(bf16[1024,256]{1,0:T(8,128)(2,1)} %collective-permute-done.3.refs_5_), channel_id=1, source_target_pairs={{0,7},{1,0},{2,1},{3,2},{4,3},{5,4},{6,5},{7,6},{8,15},{9,8},{10,9... | collective-permute-start | bytes 1572872 | tf_op jit(solution)/shard_map/ppermute | solution.py:191
  42.6 43.0 %all-to-all-start = ((bf16[32,16,768]{2,1,0:T(8,128)(2,1)}), bf16[32,16,768]{2,1,0:T(8,128)(2,1)}, u32[]{:S(2)}, u32[]{:S(2)}) async-start(bf16[32,16,768]{2,1,0:T(8,128)(2,1)} %bitcast.4), calls=%async_computation | async-start | bytes 1572864 | tf_op jit(solution)/shard_map/all_to_all | solution.py:197
  52.4 15.9 %collective-permute-start.5 = (bf16[1024,256]{1,0:T(8,128)(2,1)}, bf16[1024,256]{1,0:T(8,128)(2,1)}, u32[]{:S(2)}, u32[]{:S(2)}) collective-permute-start(bf16[1024,256]{1,0:T(8,128)(2,1)} %collective-permute-done.1.refs_3_), channel_id=1, source_target_pairs={{0,1},{1,2},{2,3},{3,4},{4,5},{5,6},{6,7},{7,0},{8,9},{9,10},{10,1... | collective-permute-start | bytes 1572872 | tf_op jit(solution)/shard_map/ppermute | solution.py:191
  52.7 15.6 %collective-permute-start.6 = (bf16[1024,256]{1,0:T(8,128)(2,1)}, bf16[1024,256]{1,0:T(8,128)(2,1)}, u32[]{:S(2)}, u32[]{:S(2)}) collective-permute-start(bf16[1024,256]{1,0:T(8,128)(2,1)} %collective-permute-done.2.refs_4_), channel_id=1, source_target_pairs={{0,7},{1,0},{2,1},{3,2},{4,3},{5,4},{6,5},{7,6},{8,15},{9,8},{10,9... | collective-permute-start | bytes 1572872 | tf_op jit(solution)/shard_map/ppermute | solution.py:191
  56.0 23.5 %collective-permute-start.8 = (bf16[1024,256]{1,0:T(8,128)(2,1)S(1)}, bf16[1024,256]{1,0:T(8,128)(2,1)}, u32[]{:S(2)}, u32[]{:S(2)}) collective-permute-start(bf16[1024,256]{1,0:T(8,128)(2,1)S(1)} %collective-permute-done.4.refs_0_), channel_id=1, source_target_pairs={{0,1},{1,2},{2,3},{3,4},{4,5},{5,6},{6,7},{7,0},{8,9},{9,10},{10,1... | collective-permute-start | bytes 1572872 | tf_op jit(solution)/shard_map/ppermute | solution.py:191
  56.0 23.5 %collective-permute-start.11 = (bf16[1024,256]{1,0:T(8,128)(2,1)S(1)}, bf16[1024,256]{1,0:T(8,128)(2,1)}, u32[]{:S(2)}, u32[]{:S(2)}) collective-permute-start(bf16[1024,256]{1,0:T(8,128)(2,1)S(1)} %collective-permute-done.7.refs_3_), channel_id=1, source_target_pairs={{0,7},{1,0},{2,1},{3,2},{4,3},{5,4},{6,5},{7,6},{8,15},{9,8},{10,9... | collective-permute-start | bytes 1572872 | tf_op jit(solution)/shard_map/ppermute | solution.py:191
  68.3 26.2 %collective-permute-start.9 = (bf16[1024,256]{1,0:T(8,128)(2,1)}, bf16[1024,256]{1,0:T(8,128)(2,1)}, u32[]{:S(2)}, u32[]{:S(2)}) collective-permute-start(bf16[1024,256]{1,0:T(8,128)(2,1)} %collective-permute-done.5.refs_1_), channel_id=1, source_target_pairs={{0,1},{1,2},{2,3},{3,4},{4,5},{5,6},{6,7},{7,0},{8,9},{9,10},{10,1... | collective-permute-start | bytes 1572872 | tf_op jit(solution)/shard_map/ppermute | solution.py:191
  68.3 26.2 %collective-permute-start.10 = (bf16[1024,256]{1,0:T(8,128)(2,1)}, bf16[1024,256]{1,0:T(8,128)(2,1)}, u32[]{:S(2)}, u32[]{:S(2)}) collective-permute-start(bf16[1024,256]{1,0:T(8,128)(2,1)} %collective-permute-done.6.refs_2_), channel_id=1, source_target_pairs={{0,7},{1,0},{2,1},{3,2},{4,3},{5,4},{6,5},{7,6},{8,15},{9,8},{10,9... | collective-permute-start | bytes 1572872 | tf_op jit(solution)/shard_map/ppermute | solution.py:191
  79.6 22.5 %collective-permute-start.12 = (bf16[1024,256]{1,0:T(8,128)(2,1)}, bf16[1024,256]{1,0:T(8,128)(2,1)}, u32[]{:S(2)}, u32[]{:S(2)}) collective-permute-start(bf16[1024,256]{1,0:T(8,128)(2,1)} %collective-permute-done.8.refs_0_), channel_id=1, source_target_pairs={{0,1},{1,2},{2,3},{3,4},{4,5},{5,6},{6,7},{7,0},{8,9},{9,10},{10,1... | collective-permute-start | bytes 1572872 | tf_op jit(solution)/shard_map/ppermute | solution.py:191
  79.6 22.5 %collective-permute-start.13 = (bf16[1024,256]{1,0:T(8,128)(2,1)}, bf16[1024,256]{1,0:T(8,128)(2,1)}, u32[]{:S(2)}, u32[]{:S(2)}) collective-permute-start(bf16[1024,256]{1,0:T(8,128)(2,1)} %collective-permute-done.11.refs_3_), channel_id=1, source_target_pairs={{0,7},{1,0},{2,1},{3,2},{4,3},{5,4},{6,5},{7,6},{8,15},{9,8},{10,9... | collective-permute-start | bytes 1572872 | tf_op jit(solution)/shard_map/ppermute | solution.py:191
  85.5 21.1 %all-to-all-start.1 = ((bf16[32,16,512]{2,1,0:T(8,128)(2,1)}), bf16[32,16,512]{2,1,0:T(8,128)(2,1)S(1)}, u32[]{:S(2)}, u32[]{:S(2)}) async-start(bf16[32,16,512]{2,1,0:T(8,128)(2,1)} %bitcast.5), calls=%async_computation.1 | async-start | bytes 1048576 | tf_op jit(solution)/shard_map/all_to_all | solution.py:197
  106.6 22.1 %all-to-all-start.2 = ((bf16[32,16,768]{2,1,0:T(8,128)(2,1)}), bf16[32,16,768]{2,1,0:T(8,128)(2,1)S(1)}, u32[]{:S(2)}, u32[]{:S(2)}) async-start(bf16[32,16,768]{2,1,0:T(8,128)(2,1)} %bitcast.6), calls=%async_computation.2 | async-start | bytes 1572864 | tf_op jit(solution)/shard_map/all_to_all | solution.py:197
  114.4 39.1 %copy-start.7 = (f32[2,8]{1,0:T(2,128)S(1)}, f32[2,8]{1,0:T(2,128)}, u32[]{:S(2)}) copy-start(f32[2,8]{1,0:T(2,128)} %param.19) | copy-start | bytes 196
  114.4 39.7 %copy-start.4 = (f32[16,2,1024]{2,1,0:T(2,128)S(1)}, f32[16,2,1024]{2,1,0:T(2,128)}, u32[]{:S(2)}) copy-start(f32[16,2,1024]{2,1,0:T(2,128)} %param.18) | copy-start | bytes 393220
  140.9 12.5 %all-to-all-start.4 = ((f32[8,2,8]{2,1,0:T(2,128)}), f32[8,2,8]{2,1,0:T(2,128)S(1)}, u32[]{:S(2)}, u32[]{:S(2)}) async-start(f32[8,2,8]{2,1,0:T(2,128)} %broadcast_in_dim.5), calls=%async_computation.4 | async-start | bytes 16384 | tf_op jit(solution)/shard_map/all_to_all | solution.py:203

commit v3 on v2

--- a/solution.py
+++ b/solution.py
@@ -149,8 +149,10 @@
     )(fill, cont, queries, queries, out_grads, out_grads, keys_values, lse, lse, delta, delta)
 
 
-def product_kernel(turned_ref, *refs):
-    *halves, out_ref = refs
+def product_kernel(offset, turned_ref, *refs):
+    halves, out_ref = refs[: len(refs) // 2 * 2], refs[-1]
+    if len(refs) % 2 == 0:
+        halves = refs[:-2]
     half = halves[0].shape[0]
     width = halves[0].shape[1]
     rows = turned_ref.shape[0]
@@ -168,23 +170,26 @@
                 NN,
                 preferred_element_type=jnp.float32,
             )
-            out_ref[r : r + chunk, i * width : (i + 1) * width] = total.astype(jnp.bfloat16)
-
-
-def product(turned, pairs):
+            first = offset + i * width
+            out_ref[r : r + chunk, first : first + width] = total.astype(jnp.bfloat16)
+
+
+def product(turned, pairs, offset=0, total=None, filled=None):
     halves = sum([list(pair) for pair in pairs], [])
+    total = total or len(pairs)
+    operands = [turned, *halves] + ([] if filled is None else [filled])
     vmem = pl.BlockSpec(memory_space=pltpu.VMEM)
+    width = halves[0].shape[1]
     return pl.pallas_call(
-        product_kernel,
-        in_specs=[vmem] * (1 + len(halves)),
+        functools.partial(product_kernel, offset * width),
+        in_specs=[vmem] * len(operands),
         out_specs=vmem,
-        out_shape=jax.ShapeDtypeStruct(
-            (turned.shape[0], len(pairs) * halves[0].shape[1]), jnp.bfloat16
-        ),
-        compiler_params=pltpu.CompilerParams(vmem_limit_bytes=32 * 1024 * 1024),
-        cost_estimate=pl.CostEstimate(flops=1000, bytes_accessed=1000, transcendentals=0),
+        out_shape=jax.ShapeDtypeStruct((turned.shape[0], total * width), jnp.bfloat16),
+        input_output_aliases={} if filled is None else {len(operands) - 1: 0},
+        compiler_params=pltpu.CompilerParams(vmem_limit_bytes=12 * 1024 * 1024),
+        cost_estimate=pl.CostEstimate(flops=int(1300000000.0*len(pairs)), bytes_accessed=1000, transcendentals=0),
         name="projection_product",
-    )(turned, *halves)
+    )(*operands)
 
 
 def shifted(array, steps, length):
@@ -237,7 +242,7 @@
     blocks = {0: list(halves)}
     right, left = list(halves), list(halves)
     far = ring // 2
-    for step in range(1, far):
+    for step in range(1, 4):
         for part in range(2):
             right[part] = shifted(right[part], 1, ring)
             left[part] = shifted(left[part], -1, ring)
@@ -246,10 +251,14 @@
     blocks[far] = [shifted(right[0], 1, ring), shifted(left[1], -1, ring)]
 
     summed = {}
-    for offsets in ((0, -1, 1), (-2, 2), (-3, 3, far)):
-        total = sum_at_owner(product(turned, [blocks[o] for o in offsets]), DP)
+
+    def keep(offsets, together):
+        total = sum_at_owner(together, DP)
         for i, o in enumerate(offsets):
             summed[o % ring] = total[:, i * 2 * HD : (i + 1) * 2 * HD]
+
+    for group in ((0, -1, 1), (-2, 2), (-3, 3, 4)):
+        keep(group, product(turned, [blocks[o] for o in group]))
 
     rows = moment_first.shape[0]
     in_turn = jnp.stack([summed[o].reshape(rows, 2, HD) for o in range(ring)], 2)
@@ -262,7 +271,7 @@
     partial_squares = jnp.sum(
         jnp.square(proj_grads).reshape(rows, 2, heads_kv, -1), axis=(0, 3)
     )
-    squares = taken_together(taken_together(partial_squares, DP), ("tensor",))
+    squares = taken_together(taken_together(partial_squares, ("dp_2", "tensor")), ("dp_0", "dp_1"))
     new_second = ADAM_TWO * moment_second + (1 - ADAM_TWO) * squares / (D * HD)
     step_size = jnp.sqrt(new_second / (1 - ADAM_TWO**2)) + ADAM_EPS
     scaled = (new_first / (1 - ADAM_ONE**2)).reshape(rows, 2, heads_kv, -1)

time: 156 us -> 148 us (0.949)
  waiting for transfers between devices: 58 us -> 51.6 us
  starting transfers between devices: 56.7 us -> 53.2 us
  blocking collectives: 10.9 us -> 13.5 us
    ppermute x14, waiting for transfers between devices: 38.8 us -> 27.8 us  [shifted(): lax.ppermute(array, 'tensor', [(i, (i + steps) % length) for i in range(l...]
    all_to_all x3, waiting for transfers between devices: 12.7 us -> 17.5 us  [sum_at_owner(): lax.all_to_all(parts, axes, split_axis=0, concat_axis=0, tiled=True)]
    all_to_all x1, blocking collectives: 10.9 us -> 13.5 us  [taken_together(): lax.all_to_all(jnp.broadcast_to(array[None], (length, *array.shape)), axe...]
    all_to_all x3, starting transfers between devices: 26.7 us -> 24.1 us  [sum_at_owner(): lax.all_to_all(parts, axes, split_axis=0, concat_axis=0, tiled=True)]
    all_to_all x1, starting transfers between devices: 5.95 us -> 3.49 us  [taken_together(): lax.all_to_all(jnp.broadcast_to(array[None], (length, *array.shape)), axe...]
  transfers between devices with their start and end apart: 18 -> 18, of which waited for: 9 -> 13; matrix products, arithmetic and copies ran while one was open for 3% -> 3% of each run, Pallas kernels for 10% -> 11%
where the time goes in v3:
time: 148 us
  starting transfers between devices  53.2 us (36%)
  waiting for transfers between devices  51.6 us (35%)
  Pallas kernels  19.3 us (13%)
  blocking collectives  13.5 us (9%)
  local copies, waits for them, and re-layouts  6.09 us (4%)
  other arithmetic  3.07 us (2%)
    ppermute x14, waiting for transfers between devices, shifted(): lax.ppermute(array, 'tensor', [(i, (i + steps) % length) for i in range(l...  27.8 us
    ppermute x14, starting transfers between devices, shifted(): lax.ppermute(array, 'tensor', [(i, (i + steps) % length) for i in range(l...  25.6 us
    all_to_all x3, starting transfers between devices, sum_at_owner(): lax.all_to_all(parts, axes, split_axis=0, concat_axis=0, tiled=True)  24.1 us
    all_to_all x3, waiting for transfers between devices, sum_at_owner(): lax.all_to_all(parts, axes, split_axis=0, concat_axis=0, tiled=True)  17.5 us
    all_to_all x1, blocking collectives, taken_together(): lax.all_to_all(jnp.broadcast_to(array[None], (length, *array.shape)), axe...  13.5 us
    pallas_call x3, Pallas kernels, product(): pl.pallas_call(functools.partial(product_kernel, offset * width), in_spec...  12.3 us
    pallas_call x2, Pallas kernels, attention(): pl.pallas_call(functools.partial(attention_kernel, first, per_step, tile_...  6.95 us
    all_to_all x1, waiting for transfers between devices, taken_together(): lax.all_to_all(jnp.broadcast_to(array[None], (length, *array.shape)), axe...  6.31 us
  transfers between devices with their start and end apart: 18, of which 13 were waited for; matrix products, arithmetic and copies ran while one was open for 3% of the time, Pallas kernels for 11%

profile of v3, /device:TPU:1, one launch (start us, length us, event | category | flops | bytes accessed | tf_op | source)
XLA Modules:
  0.0 147.7 jit_solution(8769654394821195678)
XLA Ops:
  0.6 0.0 copy-start.5
  0.6 0.0 copy-start.6
  0.7 0.0 copy-start
  0.7 0.0 copy-start.1
  0.7 0.0 copy-start.2
  0.7 0.0 copy-start.3
  0.7 1.5 %copy.28 = bf16[2048,2,128]{2,0,1:T(8,128)(2,1)S(1)} copy(bf16[2048,2,128]{2,1,0:T(2,128)(2,1)} %param.12) | data formatting | bytes 2097152 | tf_op args[2]
  2.2 0.2 dynamic-slice_reduce_fusion
  2.4 0.1 copy-done.1
  2.5 3.5 %attention_grads.2.refs_0_ = bf16[1024,256]{1,0:T(8,128)(2,1)} custom-call(s32[16]{0:T(128)S(1)} %get-tuple-element.18.fill_ref, s32[16]{0:T(128)S(1)} %get-tuple-element.17.cont_ref, bf16[2048,256]{1,0:T(8,128)(2,1)S(1)} %copy-done, bf16[2048,256]{1,0:T(8,128)(2,1)S(1)} %copy-done, bf16[2048,256]{1,0:T(8,128)(2,1)S(1)} %copy-done.1, ...), custom_call_target="tpu_custom_call" | custom-call | flops 536870912 | bytes 2621440 | tf_op jit(solution)/shard_map/attention_grads/pallas_call | solution.py:123
  6.0 2.5 %collective-permute-start = (bf16[1024,256]{1,0:T(8,128)(2,1)}, bf16[1024,256]{1,0:T(8,128)(2,1)}, u32[]{:S(2)}, u32[]{:S(2)}) collective-permute-start(bf16[1024,256]{1,0:T(8,128)(2,1)} %attention_grads.2.refs_0_), channel_id=1, source_target_pairs={{0,1},{1,2},{2,3},{3,4},{4,5},{5,6},{6,7},{7,0},{8,9},{9,10},{10,1... | collective-permute-start | bytes 1572872 | tf_op jit(solution)/shard_map/ppermute | solution.py:196
  8.5 3.5 %attention_grads.3.refs_1_ = bf16[1024,256]{1,0:T(8,128)(2,1)} custom-call(s32[16]{0:T(128)S(1)} %get-tuple-element.18.fill_ref, s32[16]{0:T(128)S(1)} %get-tuple-element.17.cont_ref, bf16[2048,256]{1,0:T(8,128)(2,1)S(1)} %copy-done, bf16[2048,256]{1,0:T(8,128)(2,1)S(1)} %copy-done, bf16[2048,256]{1,0:T(8,128)(2,1)S(1)} %copy-done.1, ...), custom_call_target="tpu_custom_call" | custom-call | flops 536870912 | bytes 2621440 | tf_op jit(solution)/shard_map/attention_grads/pallas_call | solution.py:123
  12.0 3.9 %collective-permute-start.3 = (bf16[1024,256]{1,0:T(8,128)(2,1)}, bf16[1024,256]{1,0:T(8,128)(2,1)}, u32[]{:S(2)}, u32[]{:S(2)}) collective-permute-start(bf16[1024,256]{1,0:T(8,128)(2,1)} %attention_grads.3.refs_1_), channel_id=1, source_target_pairs={{0,7},{1,0},{2,1},{3,2},{4,3},{5,4},{6,5},{7,6},{8,15},{9,8},{10,9... | collective-permute-start | bytes 1572872 | tf_op jit(solution)/shard_map/ppermute | solution.py:196
  15.9 0.0 collective-permute-start.1
  15.9 2.7 %collective-permute-start.2 = (bf16[1024,256]{1,0:T(8,128)(2,1)}, bf16[1024,256]{1,0:T(8,128)(2,1)}, u32[]{:S(2)}, u32[]{:S(2)}) collective-permute-start(bf16[1024,256]{1,0:T(8,128)(2,1)} %attention_grads.2.refs_0_), channel_id=1, source_target_pairs={{0,7},{1,0},{2,1},{3,2},{4,3},{5,4},{6,5},{7,6},{8,15},{9,8},{10,9... | collective-permute-start | bytes 1572872 | tf_op jit(solution)/shard_map/ppermute | solution.py:196
  18.6 5.8 %collective-permute-done.refs_2_ = bf16[1024,256]{1,0:T(8,128)(2,1)} collective-permute-done((bf16[1024,256]{1,0:T(8,128)(2,1)}, bf16[1024,256]{1,0:T(8,128)(2,1)}, u32[]{:S(2)}, u32[]{:S(2)}) %collective-permute-start) | collective-permute-done | bytes 524320 | tf_op jit(solution)/shard_map/ppermute | solution.py:196
  24.3 0.0 collective-permute-start.4
  24.3 2.4 %collective-permute-done.3.refs_5_ = bf16[1024,256]{1,0:T(8,128)(2,1)} collective-permute-done((bf16[1024,256]{1,0:T(8,128)(2,1)}, bf16[1024,256]{1,0:T(8,128)(2,1)}, u32[]{:S(2)}, u32[]{:S(2)}) %collective-permute-start.3) | collective-permute-done | bytes 524320 | tf_op jit(solution)/shard_map/ppermute | solution.py:196
  26.8 3.4 %collective-permute-start.7 = (bf16[1024,256]{1,0:T(8,128)(2,1)}, bf16[1024,256]{1,0:T(8,128)(2,1)}, u32[]{:S(2)}, u32[]{:S(2)}) collective-permute-start(bf16[1024,256]{1,0:T(8,128)(2,1)} %collective-permute-done.3.refs_5_), channel_id=1, source_target_pairs={{0,7},{1,0},{2,1},{3,2},{4,3},{5,4},{6,5},{7,6},{8,15},{9,8},{10,9... | collective-permute-start | bytes 1572872 | tf_op jit(solution)/shard_map/ppermute | solution.py:196
  30.2 2.9 %copy.19 = bf16[2048,512]{0,1:T(8,128)(2,1)S(1)} copy(bf16[2048,512]{1,0:T(8,128)(2,1)} %param.10) | data formatting | bytes 4194304 | tf_op args[0]
  33.1 2.5 %collective-permute-done.1.refs_3_ = bf16[1024,256]{1,0:T(8,128)(2,1)} collective-permute-done((bf16[1024,256]{1,0:T(8,128)(2,1)}, bf16[1024,256]{1,0:T(8,128)(2,1)}, u32[]{:S(2)}, u32[]{:S(2)}) %collective-permute-start.1) | collective-permute-done | bytes 524320 | tf_op jit(solution)/shard_map/ppermute | solution.py:196
  35.6 0.0 collective-permute-start.5
  35.6 2.4 %collective-permute-done.2.refs_4_ = bf16[1024,256]{1,0:T(8,128)(2,1)} collective-permute-done((bf16[1024,256]{1,0:T(8,128)(2,1)}, bf16[1024,256]{1,0:T(8,128)(2,1)}, u32[]{:S(2)}, u32[]{:S(2)}) %collective-permute-start.2) | collective-permute-done | bytes 524320 | tf_op jit(solution)/shard_map/ppermute | solution.py:196
  38.0 3.4 %collective-permute-start.6 = (bf16[1024,256]{1,0:T(8,128)(2,1)}, bf16[1024,256]{1,0:T(8,128)(2,1)}, u32[]{:S(2)}, u32[]{:S(2)}) collective-permute-start(bf16[1024,256]{1,0:T(8,128)(2,1)} %collective-permute-done.2.refs_4_), channel_id=1, source_target_pairs={{0,7},{1,0},{2,1},{3,2},{4,3},{5,4},{6,5},{7,6},{8,15},{9,8},{10,9... | collective-permute-start | bytes 1572872 | tf_op jit(solution)/shard_map/ppermute | solution.py:196
  41.4 5.3 %collective-permute-done.4.refs_0_ = bf16[1024,256]{1,0:T(8,128)(2,1)S(1)} collective-permute-done((bf16[1024,256]{1,0:T(8,128)(2,1)}, bf16[1024,256]{1,0:T(8,128)(2,1)S(1)}, u32[]{:S(2)}, u32[]{:S(2)}) %collective-permute-start.4) | collective-permute-done | bytes 524320 | tf_op jit(solution)/shard_map/ppermute | solution.py:196
  46.7 0.0 collective-permute-start.8
  46.7 2.5 %collective-permute-done.7.refs_3_ = bf16[1024,256]{1,0:T(8,128)(2,1)} collective-permute-done((bf16[1024,256]{1,0:T(8,128)(2,1)}, bf16[1024,256]{1,0:T(8,128)(2,1)}, u32[]{:S(2)}, u32[]{:S(2)}) %collective-permute-start.7) | collective-permute-done | bytes 524320 | tf_op jit(solution)/shard_map/ppermute | solution.py:196
  49.2 3.4 %collective-permute-start.11 = (bf16[1024,256]{1,0:T(8,128)(2,1)}, bf16[1024,256]{1,0:T(8,128)(2,1)}, u32[]{:S(2)}, u32[]{:S(2)}) collective-permute-start(bf16[1024,256]{1,0:T(8,128)(2,1)} %collective-permute-done.7.refs_3_), channel_id=1, source_target_pairs={{0,7},{1,0},{2,1},{3,2},{4,3},{5,4},{6,5},{7,6},{8,15},{9,8},{10,9... | collective-permute-start | bytes 1572872 | tf_op jit(solution)/shard_map/ppermute | solution.py:196
  52.6 4.5 %projection_product.3 = bf16[512,768]{1,0:T(8,128)(2,1)} custom-call(bf16[512,2048]{1,0:T(8,128)(2,1)S(1)} %bitcast.18, bf16[1024,256]{1,0:T(8,128)(2,1)} %attention_grads.2.refs_0_, bf16[1024,256]{1,0:T(8,128)(2,1)} %attention_grads.3.refs_1_, bf16[1024,256]{1,0:T(8,128)(2,1)} %collective-permute-done.refs_2_, ...), custom_call_target="tpu_custom_call" | custom-call | flops 3900000000 | bytes 1000 | tf_op jit(solution)/shard_map/projection_product/pallas_call | solution.py:183
  57.2 10.2 %all-to-all-start = ((bf16[32,16,768]{2,1,0:T(8,128)(2,1)}), bf16[32,16,768]{2,1,0:T(8,128)(2,1)}, u32[]{:S(2)}, u32[]{:S(2)}) async-start(bf16[32,16,768]{2,1,0:T(8,128)(2,1)} %bitcast.4), calls=%async_computation | async-start | bytes 1572864 | tf_op jit(solution)/shard_map/all_to_all | solution.py:202
  67.4 0.0 collective-permute-done.5.refs_1_
  67.4 0.3 collective-permute-start.9
  67.6 0.0 collective-permute-done.6.refs_2_
  67.7 2.7 %collective-permute-start.10 = (bf16[1024,256]{1,0:T(8,128)(2,1)}, bf16[1024,256]{1,0:T(8,128)(2,1)}, u32[]{:S(2)}, u32[]{:S(2)}) collective-permute-start(bf16[1024,256]{1,0:T(8,128)(2,1)} %collective-permute-done.6.refs_2_), channel_id=1, source_target_pairs={{0,7},{1,0},{2,1},{3,2},{4,3},{5,4},{6,5},{7,6},{8,15},{9,8},{10,9... | collective-permute-start | bytes 1572872 | tf_op jit(solution)/shard_map/ppermute | solution.py:196
  70.3 0.0 collective-permute-done.8.refs_0_
  70.3 0.0 collective-permute-start.12
  70.3 1.4 collective-permute-done.11.refs_3_
  71.7 3.4 %collective-permute-start.13 = (bf16[1024,256]{1,0:T(8,128)(2,1)}, bf16[1024,256]{1,0:T(8,128)(2,1)}, u32[]{:S(2)}, u32[]{:S(2)}) collective-permute-start(bf16[1024,256]{1,0:T(8,128)(2,1)} %collective-permute-done.11.refs_3_), channel_id=1, source_target_pairs={{0,7},{1,0},{2,1},{3,2},{4,3},{5,4},{6,5},{7,6},{8,15},{9,8},{10,9... | collective-permute-start | bytes 1572872 | tf_op jit(solution)/shard_map/ppermute | solution.py:196
  75.1 3.4 %projection_product.4 = bf16[512,512]{1,0:T(8,128)(2,1)} custom-call(bf16[512,2048]{1,0:T(8,128)(2,1)S(1)} %bitcast.19, bf16[1024,256]{1,0:T(8,128)(2,1)S(1)} %collective-permute-done.4.refs_0_, bf16[1024,256]{1,0:T(8,128)(2,1)} %collective-permute-done.5.refs_1_, bf16[1024,256]{1,0:T(8,128)(2,1)} %collective-permute-done.6.refs_2_, ...), custom_call_target="tpu_custom_call" | custom-call | flops 2600000000 | bytes 1000 | tf_op jit(solution)/shard_map/projection_product/pallas_call | solution.py:183
  78.5 3.1 %all-to-all-done = bf16[32,16,768]{2,1,0:T(8,128)(2,1)} async-done(((bf16[32,16,768]{2,1,0:T(8,128)(2,1)}), bf16[32,16,768]{2,1,0:T(8,128)(2,1)}, u32[]{:S(2)}, u32[]{:S(2)}) %all-to-all-start) | async-done | bytes 786464 | tf_op jit(solution)/shard_map/all_to_all | solution.py:202
  81.6 7.0 %all-to-all-start.1 = ((bf16[32,16,512]{2,1,0:T(8,128)(2,1)}), bf16[32,16,512]{2,1,0:T(8,128)(2,1)S(1)}, u32[]{:S(2)}, u32[]{:S(2)}) async-start(bf16[32,16,512]{2,1,0:T(8,128)(2,1)} %bitcast.5), calls=%async_computation.1 | async-start | bytes 1048576 | tf_op jit(solution)/shard_map/all_to_all | solution.py:202
  88.6 0.0 collective-permute-done.9.refs_1_
  88.6 0.0 collective-permute-done.10.refs_2_
  88.7 5.0 %collective-permute-done.12.refs_4_ = bf16[1024,256]{1,0:T(8,128)(2,1)} collective-permute-done((bf16[1024,256]{1,0:T(8,128)(2,1)S(1)}, bf16[1024,256]{1,0:T(8,128)(2,1)}, u32[]{:S(2)}, u32[]{:S(2)}) %collective-permute-start.12) | collective-permute-done | bytes 524320 | tf_op jit(solution)/shard_map/ppermute | solution.py:196
  93.6 0.6 collective-permute-done.13.refs_5_
  94.2 4.4 %projection_product.5 = bf16[512,768]{1,0:T(8,128)(2,1)} custom-call(bf16[512,2048]{1,0:T(8,128)(2,1)S(1)} %bitcast.20, bf16[1024,256]{1,0:T(8,128)(2,1)S(1)} %collective-permute-done.8.refs_0_, bf16[1024,256]{1,0:T(8,128)(2,1)} %collective-permute-done.9.refs_1_, bf16[1024,256]{1,0:T(8,128)(2,1)} %collective-permute-done.10.refs_2_, ...), custom_call_target="tpu_custom_call" | custom-call | flops 3900000000 | bytes 1000 | tf_op jit(solution)/shard_map/projection_product/pallas_call | solution.py:183
  98.6 1.7 %all-to-all-done.1 = bf16[32,16,512]{2,1,0:T(8,128)(2,1)S(1)} async-done(((bf16[32,16,512]{2,1,0:T(8,128)(2,1)}), bf16[32,16,512]{2,1,0:T(8,128)(2,1)S(1)}, u32[]{:S(2)}, u32[]{:S(2)}) %all-to-all-start.1) | async-done | bytes 524320 | tf_op jit(solution)/shard_map/all_to_all | solution.py:202
  100.3 7.0 %all-to-all-start.2 = ((bf16[32,16,768]{2,1,0:T(8,128)(2,1)}), bf16[32,16,768]{2,1,0:T(8,128)(2,1)S(1)}, u32[]{:S(2)}, u32[]{:S(2)}) async-start(bf16[32,16,768]{2,1,0:T(8,128)(2,1)} %bitcast.6), calls=%async_computation.2 | async-start | bytes 1572864 | tf_op jit(solution)/shard_map/all_to_all | solution.py:202
  107.2 0.0 copy-start.7
  107.2 0.0 copy-start.4
  107.3 1.3 convert_reduce_fusion.1
  108.6 0.1 convert_reduce_fusion.2
  108.8 12.6 %all-to-all-done.2 = bf16[32,16,768]{2,1,0:T(8,128)(2,1)S(1)} async-done(((bf16[32,16,768]{2,1,0:T(8,128)(2,1)}), bf16[32,16,768]{2,1,0:T(8,128)(2,1)S(1)}, u32[]{:S(2)}, u32[]{:S(2)}) %all-to-all-start.2) | async-done | bytes 786464 | tf_op jit(solution)/shard_map/all_to_all | solution.py:202
  121.4 0.1 convert_reduce_fusion
  121.6 0.4 concatenate.4
  122.0 0.1 dynamic-slice_multiply_fusion
  122.2 13.5 %all_to_all.25 = f32[16,2,8]{2,1,0:T(2,128)S(1)} all-to-all(f32[16,2,8]{2,1,0:T(2,128)S(1)} %broadcast_in_dim.4), channel_id=1, replica_groups=mesh['dp_0'=4,'dp_1'=4,'dp_2'=2,'tensor'=8] {'dp_2','tensor'}, dimensions={0} | all-to-all | bytes 2048 | tf_op jit(solution)/shard_map/all_to_all | solution.py:208
  135.7 0.6 broadcast_in_dim.5
  136.3 3.5 %all-to-all-start.4 = ((f32[16,2,8]{2,1,0:T(2,128)}), f32[16,2,8]{2,1,0:T(2,128)S(1)}, u32[]{:S(2)}, u32[]{:S(2)}) async-start(f32[16,2,8]{2,1,0:T(2,128)} %broadcast_in_dim.5), calls=%async_computation.4 | async-start | bytes 32768 | tf_op jit(solution)/shard_map/all_to_all | solution.py:208
  139.8 0.1 mul.31
  139.9 6.3 %all-to-all-done.4 = f32[16,2,8]{2,1,0:T(2,128)S(1)} async-done(((f32[16,2,8]{2,1,0:T(2,128)}), f32[16,2,8]{2,1,0:T(2,128)S(1)}, u32[]{:S(2)}, u32[]{:S(2)}) %all-to-all-start.4) | async-done | bytes 1056 | tf_op jit(solution)/shard_map/all_to_all | solution.py:208
  146.3 0.6 sqrt_add_fusion
  146.8 0.1 broadcast_bitcast_fusion
  146.9 0.8 multiply_divide_fusion
  (22 shorter events, 0.3 us)
Async XLA Ops:
  0.6 1.6 %copy-start.5 = (s32[32,16]{0,1:T(8,128)S(1)}, s32[32,16]{0,1:T(8,128)}, u32[]{:S(2)}) copy-start(s32[32,16]{0,1:T(8,128)} %param.17) | copy-start | bytes 6148
  0.6 1.6 %copy-start.6 = (s32[32,16]{0,1:T(8,128)S(1)}, s32[32,16]{0,1:T(8,128)}, u32[]{:S(2)}) copy-start(s32[32,16]{0,1:T(8,128)} %param.16) | copy-start | bytes 6148
  0.7 1.8 %copy-start = (bf16[2048,256]{1,0:T(8,128)(2,1)S(1)}, bf16[2048,256]{1,0:T(8,128)(2,1)}, u32[]{:S(2)}) copy-start(bf16[2048,256]{1,0:T(8,128)(2,1)} %q_next_ref.3) | copy-start | bytes 3145732
  0.7 1.9 %copy-start.1 = (bf16[2048,256]{1,0:T(8,128)(2,1)S(1)}, bf16[2048,256]{1,0:T(8,128)(2,1)}, u32[]{:S(2)}) copy-start(bf16[2048,256]{1,0:T(8,128)(2,1)} %do_next_ref.3) | copy-start | bytes 3145732
  0.7 1.9 %copy-start.2 = (bf16[2048,2]{0,1:T(2,128)(2,1)S(1)}, bf16[2048,2]{0,1:T(2,128)(2,1)}, u32[]{:S(2)}) copy-start(bf16[2048,2]{0,1:T(2,128)(2,1)} %param.14) | copy-start | bytes 24580
  0.7 1.8 %copy-start.3 = (bf16[2048,2]{0,1:T(2,128)(2,1)S(1)}, bf16[2048,2]{0,1:T(2,128)(2,1)}, u32[]{:S(2)}) copy-start(bf16[2048,2]{0,1:T(2,128)(2,1)} %param.15) | copy-start | bytes 24580
  6.0 18.4 %collective-permute-start = (bf16[1024,256]{1,0:T(8,128)(2,1)}, bf16[1024,256]{1,0:T(8,128)(2,1)}, u32[]{:S(2)}, u32[]{:S(2)}) collective-permute-start(bf16[1024,256]{1,0:T(8,128)(2,1)} %attention_grads.2.refs_0_), channel_id=1, source_target_pairs={{0,1},{1,2},{2,3},{3,4},{4,5},{5,6},{6,7},{7,0},{8,9},{9,10},{10,1... | collective-permute-start | bytes 1572872 | tf_op jit(solution)/shard_map/ppermute | solution.py:196
  12.0 14.8 %collective-permute-start.3 = (bf16[1024,256]{1,0:T(8,128)(2,1)}, bf16[1024,256]{1,0:T(8,128)(2,1)}, u32[]{:S(2)}, u32[]{:S(2)}) collective-permute-start(bf16[1024,256]{1,0:T(8,128)(2,1)} %attention_grads.3.refs_1_), channel_id=1, source_target_pairs={{0,7},{1,0},{2,1},{3,2},{4,3},{5,4},{6,5},{7,6},{8,15},{9,8},{10,9... | collective-permute-start | bytes 1572872 | tf_op jit(solution)/shard_map/ppermute | solution.py:196
  15.9 19.7 %collective-permute-start.1 = (bf16[1024,256]{1,0:T(8,128)(2,1)}, bf16[1024,256]{1,0:T(8,128)(2,1)}, u32[]{:S(2)}, u32[]{:S(2)}) collective-permute-start(bf16[1024,256]{1,0:T(8,128)(2,1)} %attention_grads.3.refs_1_), channel_id=1, source_target_pairs={{0,1},{1,2},{2,3},{3,4},{4,5},{5,6},{6,7},{7,0},{8,9},{9,10},{10,1... | collective-permute-start | bytes 1572872 | tf_op jit(solution)/shard_map/ppermute | solution.py:196
  15.9 22.1 %collective-permute-start.2 = (bf16[1024,256]{1,0:T(8,128)(2,1)}, bf16[1024,256]{1,0:T(8,128)(2,1)}, u32[]{:S(2)}, u32[]{:S(2)}) collective-permute-start(bf16[1024,256]{1,0:T(8,128)(2,1)} %attention_grads.2.refs_0_), channel_id=1, source_target_pairs={{0,7},{1,0},{2,1},{3,2},{4,3},{5,4},{6,5},{7,6},{8,15},{9,8},{10,9... | collective-permute-start | bytes 1572872 | tf_op jit(solution)/shard_map/ppermute | solution.py:196
  24.3 22.4 %collective-permute-start.4 = (bf16[1024,256]{1,0:T(8,128)(2,1)}, bf16[1024,256]{1,0:T(8,128)(2,1)S(1)}, u32[]{:S(2)}, u32[]{:S(2)}) collective-permute-start(bf16[1024,256]{1,0:T(8,128)(2,1)} %collective-permute-done.refs_2_), channel_id=1, source_target_pairs={{0,1},{1,2},{2,3},{3,4},{4,5},{5,6},{6,7},{7,0},{8,9},{9,10},{10,1... | collective-permute-start | bytes 1572872 | tf_op jit(solution)/shard_map/ppermute | solution.py:196
  26.8 22.5 %collective-permute-start.7 = (bf16[1024,256]{1,0:T(8,128)(2,1)}, bf16[1024,256]{1,0:T(8,128)(2,1)}, u32[]{:S(2)}, u32[]{:S(2)}) collective-permute-start(bf16[1024,256]{1,0:T(8,128)(2,1)} %collective-permute-done.3.refs_5_), channel_id=1, source_target_pairs={{0,7},{1,0},{2,1},{3,2},{4,3},{5,4},{6,5},{7,6},{8,15},{9,8},{10,9... | collective-permute-start | bytes 1572872 | tf_op jit(solution)/shard_map/ppermute | solution.py:196
  35.6 31.8 %collective-permute-start.5 = (bf16[1024,256]{1,0:T(8,128)(2,1)}, bf16[1024,256]{1,0:T(8,128)(2,1)}, u32[]{:S(2)}, u32[]{:S(2)}) collective-permute-start(bf16[1024,256]{1,0:T(8,128)(2,1)} %collective-permute-done.1.refs_3_), channel_id=1, source_target_pairs={{0,1},{1,2},{2,3},{3,4},{4,5},{5,6},{6,7},{7,0},{8,9},{9,10},{10,1... | collective-permute-start | bytes 1572872 | tf_op jit(solution)/shard_map/ppermute | solution.py:196
  38.0 29.6 %collective-permute-start.6 = (bf16[1024,256]{1,0:T(8,128)(2,1)}, bf16[1024,256]{1,0:T(8,128)(2,1)}, u32[]{:S(2)}, u32[]{:S(2)}) collective-permute-start(bf16[1024,256]{1,0:T(8,128)(2,1)} %collective-permute-done.2.refs_4_), channel_id=1, source_target_pairs={{0,7},{1,0},{2,1},{3,2},{4,3},{5,4},{6,5},{7,6},{8,15},{9,8},{10,9... | collective-permute-start | bytes 1572872 | tf_op jit(solution)/shard_map/ppermute | solution.py:196
  46.7 23.6 %collective-permute-start.8 = (bf16[1024,256]{1,0:T(8,128)(2,1)S(1)}, bf16[1024,256]{1,0:T(8,128)(2,1)S(1)}, u32[]{:S(2)}, u32[]{:S(2)}) collective-permute-start(bf16[1024,256]{1,0:T(8,128)(2,1)S(1)} %collective-permute-done.4.refs_0_), channel_id=1, source_target_pairs={{0,1},{1,2},{2,3},{3,4},{4,5},{5,6},{6,7},{7,0},{8,9},{9,10},{10,1... | collective-permute-start | bytes 1572872 | tf_op jit(solution)/shard_map/ppermute | solution.py:196
  49.2 22.5 %collective-permute-start.11 = (bf16[1024,256]{1,0:T(8,128)(2,1)}, bf16[1024,256]{1,0:T(8,128)(2,1)}, u32[]{:S(2)}, u32[]{:S(2)}) collective-permute-start(bf16[1024,256]{1,0:T(8,128)(2,1)} %collective-permute-done.7.refs_3_), channel_id=1, source_target_pairs={{0,7},{1,0},{2,1},{3,2},{4,3},{5,4},{6,5},{7,6},{8,15},{9,8},{10,9... | collective-permute-start | bytes 1572872 | tf_op jit(solution)/shard_map/ppermute | solution.py:196
  57.2 24.5 %all-to-all-start = ((bf16[32,16,768]{2,1,0:T(8,128)(2,1)}), bf16[32,16,768]{2,1,0:T(8,128)(2,1)}, u32[]{:S(2)}, u32[]{:S(2)}) async-start(bf16[32,16,768]{2,1,0:T(8,128)(2,1)} %bitcast.4), calls=%async_computation | async-start | bytes 1572864 | tf_op jit(solution)/shard_map/all_to_all | solution.py:202
  67.4 21.3 %collective-permute-start.9 = (bf16[1024,256]{1,0:T(8,128)(2,1)}, bf16[1024,256]{1,0:T(8,128)(2,1)}, u32[]{:S(2)}, u32[]{:S(2)}) collective-permute-start(bf16[1024,256]{1,0:T(8,128)(2,1)} %collective-permute-done.5.refs_1_), channel_id=1, source_target_pairs={{0,1},{1,2},{2,3},{3,4},{4,5},{5,6},{6,7},{7,0},{8,9},{9,10},{10,1... | collective-permute-start | bytes 1572872 | tf_op jit(solution)/shard_map/ppermute | solution.py:196
  67.7 21.0 %collective-permute-start.10 = (bf16[1024,256]{1,0:T(8,128)(2,1)}, bf16[1024,256]{1,0:T(8,128)(2,1)}, u32[]{:S(2)}, u32[]{:S(2)}) collective-permute-start(bf16[1024,256]{1,0:T(8,128)(2,1)} %collective-permute-done.6.refs_2_), channel_id=1, source_target_pairs={{0,7},{1,0},{2,1},{3,2},{4,3},{5,4},{6,5},{7,6},{8,15},{9,8},{10,9... | collective-permute-start | bytes 1572872 | tf_op jit(solution)/shard_map/ppermute | solution.py:196
  70.3 23.3 %collective-permute-start.12 = (bf16[1024,256]{1,0:T(8,128)(2,1)S(1)}, bf16[1024,256]{1,0:T(8,128)(2,1)}, u32[]{:S(2)}, u32[]{:S(2)}) collective-permute-start(bf16[1024,256]{1,0:T(8,128)(2,1)S(1)} %collective-permute-done.8.refs_0_), channel_id=1, source_target_pairs={{0,1},{1,2},{2,3},{3,4},{4,5},{5,6},{6,7},{7,0},{8,9},{9,10},{10,1... | collective-permute-start | bytes 1572872 | tf_op jit(solution)/shard_map/ppermute | solution.py:196
  71.7 22.5 %collective-permute-start.13 = (bf16[1024,256]{1,0:T(8,128)(2,1)}, bf16[1024,256]{1,0:T(8,128)(2,1)}, u32[]{:S(2)}, u32[]{:S(2)}) collective-permute-start(bf16[1024,256]{1,0:T(8,128)(2,1)} %collective-permute-done.11.refs_3_), channel_id=1, source_target_pairs={{0,7},{1,0},{2,1},{3,2},{4,3},{5,4},{6,5},{7,6},{8,15},{9,8},{10,9... | collective-permute-start | bytes 1572872 | tf_op jit(solution)/shard_map/ppermute | solution.py:196
  81.6 18.6 %all-to-all-start.1 = ((bf16[32,16,512]{2,1,0:T(8,128)(2,1)}), bf16[32,16,512]{2,1,0:T(8,128)(2,1)S(1)}, u32[]{:S(2)}, u32[]{:S(2)}) async-start(bf16[32,16,512]{2,1,0:T(8,128)(2,1)} %bitcast.5), calls=%async_computation.1 | async-start | bytes 1048576 | tf_op jit(solution)/shard_map/all_to_all | solution.py:202
  100.3 21.2 %all-to-all-start.2 = ((bf16[32,16,768]{2,1,0:T(8,128)(2,1)}), bf16[32,16,768]{2,1,0:T(8,128)(2,1)S(1)}, u32[]{:S(2)}, u32[]{:S(2)}) async-start(bf16[32,16,768]{2,1,0:T(8,128)(2,1)} %bitcast.6), calls=%async_computation.2 | async-start | bytes 1572864 | tf_op jit(solution)/shard_map/all_to_all | solution.py:202
  107.2 39.0 %copy-start.7 = (f32[2,8]{1,0:T(2,128)S(1)}, f32[2,8]{1,0:T(2,128)}, u32[]{:S(2)}) copy-start(f32[2,8]{1,0:T(2,128)} %param.19) | copy-start | bytes 196
  107.2 39.7 %copy-start.4 = (f32[16,2,1024]{2,1,0:T(2,128)S(1)}, f32[16,2,1024]{2,1,0:T(2,128)}, u32[]{:S(2)}) copy-start(f32[16,2,1024]{2,1,0:T(2,128)} %param.18) | copy-start | bytes 393220
  136.3 9.9 %all-to-all-start.4 = ((f32[16,2,8]{2,1,0:T(2,128)}), f32[16,2,8]{2,1,0:T(2,128)S(1)}, u32[]{:S(2)}, u32[]{:S(2)}) async-start(f32[16,2,8]{2,1,0:T(2,128)} %broadcast_in_dim.5), calls=%async_computation.4 | async-start | bytes 32768 | tf_op jit(solution)/shard_map/all_to_all | solution.py:208

commit v4 on v3

--- a/solution.py
+++ b/solution.py
@@ -130,7 +130,7 @@
                 pl.BlockSpec((BLK, width), follow),
                 pl.BlockSpec((rows, width), own),
                 pl.BlockSpec((BLK, width), follow),
-                pl.BlockSpec((2, rows, HD), lambda i, *_: (0, offset + i, 0)),
+                pl.BlockSpec((2, rows, HD), lambda i, *_: (0, i, 0)),
                 pl.BlockSpec((heads, rows), own_lanes),
                 pl.BlockSpec((heads, BLK), follow_lanes),
                 pl.BlockSpec((heads, rows), own_lanes),
@@ -156,7 +156,7 @@
     half = halves[0].shape[0]
     width = halves[0].shape[1]
     rows = turned_ref.shape[0]
-    chunk = 256
+    chunk = rows
     for i in range(len(halves) // 2):
         for r in range(0, rows, chunk):
             total = lax.dot_general(
@@ -187,7 +187,7 @@
         out_shape=jax.ShapeDtypeStruct((turned.shape[0], total * width), jnp.bfloat16),
         input_output_aliases={} if filled is None else {len(operands) - 1: 0},
         compiler_params=pltpu.CompilerParams(vmem_limit_bytes=12 * 1024 * 1024),
-        cost_estimate=pl.CostEstimate(flops=int(1300000000.0*len(pairs)), bytes_accessed=1000, transcendentals=0),
+        cost_estimate=pl.CostEstimate(flops=1300000000 * len(pairs), bytes_accessed=1000, transcendentals=0),
         name="projection_product",
     )(*operands)
 
@@ -231,10 +231,9 @@
     place = lax.axis_index("tensor")
     fill = lax.dynamic_index_in_dim(tile_fill, my_group, 0, keepdims=False)
     cont = lax.dynamic_index_in_dim(tile_cont, my_group, 0, keepdims=False)
-    kv = jnp.swapaxes(keys_values, 0, 1)
     half = tile_count // 2
     halves = [
-        attention(first, half, 4, fill, cont, queries, out_grads, kv, log_sums.T, deltas.T)
+        attention(first, half, 8, fill, cont, queries, out_grads, jnp.swapaxes(keys_values[first * BLK : (first + half) * BLK], 0, 1), log_sums.T, deltas.T)
         for first in (0, half)
     ]
     turned = layer_input.T

time: 148 us -> 148 us (level)
  Pallas kernels: 19.3 us -> 17.1 us
    slice x0 -> x1, local copies, waits for them, and re-layouts: none -> 2.86 us  [per_device(): keys_values[first * BLK:(first + half) * BLK]]
    pallas_call x2, Pallas kernels: 6.95 us -> 5.07 us  [attention(): pl.pallas_call(functools.partial(attention_kernel, first, per_step, tile_...]
    unnamed x20 -> x23, local copies, waits for them, and re-layouts: 4.64 us -> 3.19 us
  transfers between devices with their start and end apart: 18 -> 18, of which waited for: 13 -> 14; matrix products, arithmetic and copies ran while one was open for 3% -> 4% of each run, Pallas kernels for 11% -> 10%
where the time goes in v4:
time: 148 us; the launch traced here: 147 us
  starting transfers between devices  53.6 us (36%)
  waiting for transfers between devices  50.4 us (34%)
  Pallas kernels  17.1 us (12%)
  blocking collectives  13.5 us (9%)
  local copies, waits for them, and re-layouts  7.49 us (5%)
  other arithmetic  4.12 us (3%)
    ppermute x14, waiting for transfers between devices, shifted(): lax.ppermute(array, 'tensor', [(i, (i + steps) % length) for i in range(l...  27.8 us
    ppermute x14, starting transfers between devices, shifted(): lax.ppermute(array, 'tensor', [(i, (i + steps) % length) for i in range(l...  25.9 us
    all_to_all x3, starting transfers between devices, sum_at_owner(): lax.all_to_all(parts, axes, split_axis=0, concat_axis=0, tiled=True)  24.2 us
    all_to_all x3, waiting for transfers between devices, sum_at_owner(): lax.all_to_all(parts, axes, split_axis=0, concat_axis=0, tiled=True)  16.3 us
    all_to_all x1, blocking collectives, taken_together(): lax.all_to_all(jnp.broadcast_to(array[None], (length, *array.shape)), axe...  13.5 us
    pallas_call x3, Pallas kernels, product(): pl.pallas_call(functools.partial(product_kernel, offset * width), in_spec...  12 us
    all_to_all x1, waiting for transfers between devices, taken_together(): lax.all_to_all(jnp.broadcast_to(array[None], (length, *array.shape)), axe...  6.31 us
    pallas_call x2, Pallas kernels, attention(): pl.pallas_call(functools.partial(attention_kernel, first, per_step, tile_...  5.07 us
  transfers between devices with their start and end apart: 18, of which 14 were waited for; matrix products, arithmetic and copies ran while one was open for 4% of the time, Pallas kernels for 10%

profile of v4, /device:TPU:1, one launch (start us, length us, event | category | flops | bytes accessed | tf_op | source)
XLA Modules:
  0.0 147.1 jit_solution(14556709169377243163)
XLA Ops:
  0.6 0.0 copy-start.6
  0.6 0.0 copy-start.7
  0.7 0.0 copy-start
  0.7 0.0 copy-start.1
  0.7 0.0 copy-start.2
  0.7 2.9 %fusion = (bf16[1024,2,128]{2,1,0:T(2,128)(2,1)}, bf16[1024,2,128]{2,1,0:T(2,128)(2,1)S(1)}) fusion(bf16[2048,2,128]{2,1,0:T(2,128)(2,1)} %param.12), kind=kLoop, calls=%fused_computation.15 | loop fusion | bytes 2097152 | tf_op jit(solution)/shard_map/slice | solution.py:236
  3.6 0.1 copy.36
  3.7 0.2 dynamic-slice_reduce_fusion
  3.9 2.5 %attention_grads.2.refs_0_ = bf16[1024,256]{1,0:T(8,128)(2,1)S(1)} custom-call(s32[16]{0:T(128)S(1)} %get-tuple-element.20.fill_ref, s32[16]{0:T(128)S(1)} %get-tuple-element.19.cont_ref, bf16[2048,256]{1,0:T(8,128)(2,1)S(1)} %copy-done, bf16[2048,256]{1,0:T(8,128)(2,1)S(1)} %copy-done, bf16[2048,256]{1,0:T(8,128)(2,1)S(1)} %copy-done.1, ...), custom_call_target="tpu_custom_call" | custom-call | flops 536870912 | bytes 2621440 | tf_op jit(solution)/shard_map/attention_grads/pallas_call | solution.py:123
  6.4 2.5 %collective-permute-start = (bf16[1024,256]{1,0:T(8,128)(2,1)S(1)}, bf16[1024,256]{1,0:T(8,128)(2,1)}, u32[]{:S(2)}, u32[]{:S(2)}) collective-permute-start(bf16[1024,256]{1,0:T(8,128)(2,1)S(1)} %attention_grads.2.refs_0_), channel_id=1, source_target_pairs={{0,1},{1,2},{2,3},{3,4},{4,5},{5,6},{6,7},{7,0},{8,9},{9,10},{10,1... | collective-permute-start | bytes 1572872 | tf_op jit(solution)/shard_map/ppermute | solution.py:196
  9.0 0.1 copy.35
  9.0 2.5 %attention_grads.3.refs_1_ = bf16[1024,256]{1,0:T(8,128)(2,1)S(1)} custom-call(s32[16]{0:T(128)S(1)} %get-tuple-element.20.fill_ref, s32[16]{0:T(128)S(1)} %get-tuple-element.19.cont_ref, bf16[2048,256]{1,0:T(8,128)(2,1)S(1)} %copy-done, bf16[2048,256]{1,0:T(8,128)(2,1)S(1)} %copy-done, bf16[2048,256]{1,0:T(8,128)(2,1)S(1)} %copy-done.1, ...), custom_call_target="tpu_custom_call" | custom-call | flops 536870912 | bytes 2621440 | tf_op jit(solution)/shard_map/attention_grads/pallas_call | solution.py:123
  11.6 4.0 %collective-permute-start.3 = (bf16[1024,256]{1,0:T(8,128)(2,1)S(1)}, bf16[1024,256]{1,0:T(8,128)(2,1)}, u32[]{:S(2)}, u32[]{:S(2)}) collective-permute-start(bf16[1024,256]{1,0:T(8,128)(2,1)S(1)} %attention_grads.3.refs_1_), channel_id=1, source_target_pairs={{0,7},{1,0},{2,1},{3,2},{4,3},{5,4},{6,5},{7,6},{8,15},{9,8},{10,9... | collective-permute-start | bytes 1572872 | tf_op jit(solution)/shard_map/ppermute | solution.py:196
  15.6 0.0 collective-permute-start.1
  15.6 2.7 %collective-permute-start.2 = (bf16[1024,256]{1,0:T(8,128)(2,1)S(1)}, bf16[1024,256]{1,0:T(8,128)(2,1)}, u32[]{:S(2)}, u32[]{:S(2)}) collective-permute-start(bf16[1024,256]{1,0:T(8,128)(2,1)S(1)} %attention_grads.2.refs_0_), channel_id=1, source_target_pairs={{0,7},{1,0},{2,1},{3,2},{4,3},{5,4},{6,5},{7,6},{8,15},{9,8},{10,9... | collective-permute-start | bytes 1572872 | tf_op jit(solution)/shard_map/ppermute | solution.py:196
  18.3 6.3 %collective-permute-done.refs_2_ = bf16[1024,256]{1,0:T(8,128)(2,1)} collective-permute-done((bf16[1024,256]{1,0:T(8,128)(2,1)S(1)}, bf16[1024,256]{1,0:T(8,128)(2,1)}, u32[]{:S(2)}, u32[]{:S(2)}) %collective-permute-start) | collective-permute-done | bytes 524320 | tf_op jit(solution)/shard_map/ppermute | solution.py:196
  24.7 0.0 collective-permute-start.4
  24.7 1.6 %collective-permute-done.3.refs_5_ = bf16[1024,256]{1,0:T(8,128)(2,1)} collective-permute-done((bf16[1024,256]{1,0:T(8,128)(2,1)S(1)}, bf16[1024,256]{1,0:T(8,128)(2,1)}, u32[]{:S(2)}, u32[]{:S(2)}) %collective-permute-start.3) | collective-permute-done | bytes 524320 | tf_op jit(solution)/shard_map/ppermute | solution.py:196
  26.2 3.5 %collective-permute-start.7 = (bf16[1024,256]{1,0:T(8,128)(2,1)}, bf16[1024,256]{1,0:T(8,128)(2,1)}, u32[]{:S(2)}, u32[]{:S(2)}) collective-permute-start(bf16[1024,256]{1,0:T(8,128)(2,1)} %collective-permute-done.3.refs_5_), channel_id=1, source_target_pairs={{0,7},{1,0},{2,1},{3,2},{4,3},{5,4},{6,5},{7,6},{8,15},{9,8},{10,9... | collective-permute-start | bytes 1572872 | tf_op jit(solution)/shard_map/ppermute | solution.py:196
  29.7 2.9 %copy.22 = bf16[2048,512]{0,1:T(8,128)(2,1)S(1)} copy(bf16[2048,512]{1,0:T(8,128)(2,1)} %param.10) | data formatting | bytes 4194304 | tf_op args[0]
  32.7 3.2 %collective-permute-done.1.refs_3_ = bf16[1024,256]{1,0:T(8,128)(2,1)} collective-permute-done((bf16[1024,256]{1,0:T(8,128)(2,1)S(1)}, bf16[1024,256]{1,0:T(8,128)(2,1)}, u32[]{:S(2)}, u32[]{:S(2)}) %collective-permute-start.1) | collective-permute-done | bytes 524320 | tf_op jit(solution)/shard_map/ppermute | solution.py:196
  35.9 0.0 collective-permute-start.5
  35.9 1.6 %collective-permute-done.2.refs_4_ = bf16[1024,256]{1,0:T(8,128)(2,1)} collective-permute-done((bf16[1024,256]{1,0:T(8,128)(2,1)S(1)}, bf16[1024,256]{1,0:T(8,128)(2,1)}, u32[]{:S(2)}, u32[]{:S(2)}) %collective-permute-start.2) | collective-permute-done | bytes 524320 | tf_op jit(solution)/shard_map/ppermute | solution.py:196
  37.5 3.5 %collective-permute-start.6 = (bf16[1024,256]{1,0:T(8,128)(2,1)}, bf16[1024,256]{1,0:T(8,128)(2,1)}, u32[]{:S(2)}, u32[]{:S(2)}) collective-permute-start(bf16[1024,256]{1,0:T(8,128)(2,1)} %collective-permute-done.2.refs_4_), channel_id=1, source_target_pairs={{0,7},{1,0},{2,1},{3,2},{4,3},{5,4},{6,5},{7,6},{8,15},{9,8},{10,9... | collective-permute-start | bytes 1572872 | tf_op jit(solution)/shard_map/ppermute | solution.py:196
  41.0 6.2 %collective-permute-done.4.refs_0_ = bf16[1024,256]{1,0:T(8,128)(2,1)} collective-permute-done((bf16[1024,256]{1,0:T(8,128)(2,1)}, bf16[1024,256]{1,0:T(8,128)(2,1)}, u32[]{:S(2)}, u32[]{:S(2)}) %collective-permute-start.4) | collective-permute-done | bytes 524320 | tf_op jit(solution)/shard_map/ppermute | solution.py:196
  47.1 0.0 collective-permute-start.8
  47.1 1.7 %collective-permute-done.7.refs_3_ = bf16[1024,256]{1,0:T(8,128)(2,1)} collective-permute-done((bf16[1024,256]{1,0:T(8,128)(2,1)}, bf16[1024,256]{1,0:T(8,128)(2,1)}, u32[]{:S(2)}, u32[]{:S(2)}) %collective-permute-start.7) | collective-permute-done | bytes 524320 | tf_op jit(solution)/shard_map/ppermute | solution.py:196
  48.8 3.4 %collective-permute-start.11 = (bf16[1024,256]{1,0:T(8,128)(2,1)}, bf16[1024,256]{1,0:T(8,128)(2,1)}, u32[]{:S(2)}, u32[]{:S(2)}) collective-permute-start(bf16[1024,256]{1,0:T(8,128)(2,1)} %collective-permute-done.7.refs_3_), channel_id=1, source_target_pairs={{0,7},{1,0},{2,1},{3,2},{4,3},{5,4},{6,5},{7,6},{8,15},{9,8},{10,9... | collective-permute-start | bytes 1572872 | tf_op jit(solution)/shard_map/ppermute | solution.py:196
  52.2 4.2 %projection_product.3 = bf16[512,768]{1,0:T(8,128)(2,1)} custom-call(bf16[512,2048]{1,0:T(8,128)(2,1)S(1)} %bitcast.21, bf16[1024,256]{1,0:T(8,128)(2,1)S(1)} %attention_grads.2.refs_0_, bf16[1024,256]{1,0:T(8,128)(2,1)S(1)} %attention_grads.3.refs_1_, bf16[1024,256]{1,0:T(8,128)(2,1)} %collective-permute-done.refs_2_, ...), custom_call_target="tpu_custom_call" | custom-call | flops 3900000000 | bytes 1000 | tf_op jit(solution)/shard_map/projection_product/pallas_call | solution.py:183
  56.4 10.1 %all-to-all-start = ((bf16[32,16,768]{2,1,0:T(8,128)(2,1)}), bf16[32,16,768]{2,1,0:T(8,128)(2,1)}, u32[]{:S(2)}, u32[]{:S(2)}) async-start(bf16[32,16,768]{2,1,0:T(8,128)(2,1)} %bitcast.5), calls=%async_computation | async-start | bytes 1572864 | tf_op jit(solution)/shard_map/all_to_all | solution.py:202
  66.6 0.0 collective-permute-done.5.refs_1_
  66.6 0.1 collective-permute-start.9
  66.7 0.0 collective-permute-done.6.refs_2_
  66.7 2.7 %collective-permute-start.10 = (bf16[1024,256]{1,0:T(8,128)(2,1)}, bf16[1024,256]{1,0:T(8,128)(2,1)S(1)}, u32[]{:S(2)}, u32[]{:S(2)}) collective-permute-start(bf16[1024,256]{1,0:T(8,128)(2,1)} %collective-permute-done.6.refs_2_), channel_id=1, source_target_pairs={{0,7},{1,0},{2,1},{3,2},{4,3},{5,4},{6,5},{7,6},{8,15},{9,8},{10,9... | collective-permute-start | bytes 1572872 | tf_op jit(solution)/shard_map/ppermute | solution.py:196
  69.3 0.3 collective-permute-done.8.refs_0_
  69.6 0.0 collective-permute-start.12
  69.6 1.7 %collective-permute-done.11.refs_3_ = bf16[1024,256]{1,0:T(8,128)(2,1)} collective-permute-done((bf16[1024,256]{1,0:T(8,128)(2,1)}, bf16[1024,256]{1,0:T(8,128)(2,1)}, u32[]{:S(2)}, u32[]{:S(2)}) %collective-permute-start.11) | collective-permute-done | bytes 524320 | tf_op jit(solution)/shard_map/ppermute | solution.py:196
  71.3 3.4 %collective-permute-start.13 = (bf16[1024,256]{1,0:T(8,128)(2,1)}, bf16[1024,256]{1,0:T(8,128)(2,1)}, u32[]{:S(2)}, u32[]{:S(2)}) collective-permute-start(bf16[1024,256]{1,0:T(8,128)(2,1)} %collective-permute-done.11.refs_3_), channel_id=1, source_target_pairs={{0,7},{1,0},{2,1},{3,2},{4,3},{5,4},{6,5},{7,6},{8,15},{9,8},{10,9... | collective-permute-start | bytes 1572872 | tf_op jit(solution)/shard_map/ppermute | solution.py:196
  74.7 3.6 %projection_product.4 = bf16[512,512]{1,0:T(8,128)(2,1)} custom-call(bf16[512,2048]{1,0:T(8,128)(2,1)S(1)} %bitcast.22, bf16[1024,256]{1,0:T(8,128)(2,1)} %collective-permute-done.4.refs_0_, bf16[1024,256]{1,0:T(8,128)(2,1)} %collective-permute-done.5.refs_1_, bf16[1024,256]{1,0:T(8,128)(2,1)} %collective-permute-done.6.refs_2_, ...), custom_call_target="tpu_custom_call" | custom-call | flops 2600000000 | bytes 1000 | tf_op jit(solution)/shard_map/projection_product/pallas_call | solution.py:183
  78.3 2.6 %all-to-all-done = bf16[32,16,768]{2,1,0:T(8,128)(2,1)} async-done(((bf16[32,16,768]{2,1,0:T(8,128)(2,1)}), bf16[32,16,768]{2,1,0:T(8,128)(2,1)}, u32[]{:S(2)}, u32[]{:S(2)}) %all-to-all-start) | async-done | bytes 786464 | tf_op jit(solution)/shard_map/all_to_all | solution.py:202
  80.9 7.5 %all-to-all-start.1 = ((bf16[32,16,512]{2,1,0:T(8,128)(2,1)}), bf16[32,16,512]{2,1,0:T(8,128)(2,1)}, u32[]{:S(2)}, u32[]{:S(2)}) async-start(bf16[32,16,512]{2,1,0:T(8,128)(2,1)} %bitcast.6), calls=%async_computation.1 | async-start | bytes 1048576 | tf_op jit(solution)/shard_map/all_to_all | solution.py:202
  88.4 0.0 collective-permute-done.9.refs_1_
  88.4 0.0 collective-permute-done.10.refs_2_
  88.4 4.2 %collective-permute-done.12.refs_4_ = bf16[1024,256]{1,0:T(8,128)(2,1)} collective-permute-done((bf16[1024,256]{1,0:T(8,128)(2,1)}, bf16[1024,256]{1,0:T(8,128)(2,1)}, u32[]{:S(2)}, u32[]{:S(2)}) %collective-permute-start.12) | collective-permute-done | bytes 524320 | tf_op jit(solution)/shard_map/ppermute | solution.py:196
  92.6 1.1 collective-permute-done.13.refs_5_
  93.7 4.2 %projection_product.5 = bf16[512,768]{1,0:T(8,128)(2,1)} custom-call(bf16[512,2048]{1,0:T(8,128)(2,1)S(1)} %bitcast.23, bf16[1024,256]{1,0:T(8,128)(2,1)} %collective-permute-done.8.refs_0_, bf16[1024,256]{1,0:T(8,128)(2,1)S(1)} %collective-permute-done.9.refs_1_, bf16[1024,256]{1,0:T(8,128)(2,1)S(1)} %collective-permute-done.10.refs_2_, ...), custom_call_target="tpu_custom_call" | custom-call | flops 3900000000 | bytes 1000 | tf_op jit(solution)/shard_map/projection_product/pallas_call | solution.py:183
  98.0 2.1 %all-to-all-done.1 = bf16[32,16,512]{2,1,0:T(8,128)(2,1)} async-done(((bf16[32,16,512]{2,1,0:T(8,128)(2,1)}), bf16[32,16,512]{2,1,0:T(8,128)(2,1)}, u32[]{:S(2)}, u32[]{:S(2)}) %all-to-all-start.1) | async-done | bytes 524320 | tf_op jit(solution)/shard_map/all_to_all | solution.py:202
  100.1 6.6 %all-to-all-start.2 = ((bf16[32,16,768]{2,1,0:T(8,128)(2,1)}), bf16[32,16,768]{2,1,0:T(8,128)(2,1)S(1)}, u32[]{:S(2)}, u32[]{:S(2)}) async-start(bf16[32,16,768]{2,1,0:T(8,128)(2,1)} %bitcast.7), calls=%async_computation.2 | async-start | bytes 1572864 | tf_op jit(solution)/shard_map/all_to_all | solution.py:202
  106.6 0.0 copy-start.8
  106.6 0.0 copy-start.5
  106.7 1.3 convert_reduce_fusion.1
  108.0 1.1 convert_reduce_fusion.2
  109.2 11.6 %all-to-all-done.2 = bf16[32,16,768]{2,1,0:T(8,128)(2,1)S(1)} async-done(((bf16[32,16,768]{2,1,0:T(8,128)(2,1)}), bf16[32,16,768]{2,1,0:T(8,128)(2,1)S(1)}, u32[]{:S(2)}, u32[]{:S(2)}) %all-to-all-start.2) | async-done | bytes 786464 | tf_op jit(solution)/shard_map/all_to_all | solution.py:202
  120.8 0.1 convert_reduce_fusion
  121.1 0.4 concatenate.4
  121.4 0.1 dynamic-slice_multiply_fusion
  121.6 13.5 %all_to_all.25 = f32[16,2,8]{2,1,0:T(2,128)S(1)} all-to-all(f32[16,2,8]{2,1,0:T(2,128)S(1)} %broadcast_in_dim.4), channel_id=1, replica_groups=mesh['dp_0'=4,'dp_1'=4,'dp_2'=2,'tensor'=8] {'dp_2','tensor'}, dimensions={0} | all-to-all | bytes 2048 | tf_op jit(solution)/shard_map/all_to_all | solution.py:208
  135.1 0.6 broadcast_in_dim.5
  135.7 3.5 %all-to-all-start.4 = ((f32[16,2,8]{2,1,0:T(2,128)}), f32[16,2,8]{2,1,0:T(2,128)S(1)}, u32[]{:S(2)}, u32[]{:S(2)}) async-start(f32[16,2,8]{2,1,0:T(2,128)} %broadcast_in_dim.5), calls=%async_computation.4 | async-start | bytes 32768 | tf_op jit(solution)/shard_map/all_to_all | solution.py:208
  139.2 0.1 mul.31
  139.3 6.3 %all-to-all-done.4 = f32[16,2,8]{2,1,0:T(2,128)S(1)} async-done(((f32[16,2,8]{2,1,0:T(2,128)}), f32[16,2,8]{2,1,0:T(2,128)S(1)}, u32[]{:S(2)}, u32[]{:S(2)}) %all-to-all-start.4) | async-done | bytes 1056 | tf_op jit(solution)/shard_map/all_to_all | solution.py:208
  145.6 0.6 sqrt_add_fusion
  146.2 0.1 broadcast_bitcast_fusion
  146.3 0.8 multiply_divide_fusion
  (26 shorter events, 0.3 us)
Async XLA Ops:
  0.6 3.0 %copy-start.6 = (s32[32,16]{0,1:T(8,128)S(1)}, s32[32,16]{0,1:T(8,128)}, u32[]{:S(2)}) copy-start(s32[32,16]{0,1:T(8,128)} %param.17) | copy-start | bytes 6148
  0.6 3.0 %copy-start.7 = (s32[32,16]{0,1:T(8,128)S(1)}, s32[32,16]{0,1:T(8,128)}, u32[]{:S(2)}) copy-start(s32[32,16]{0,1:T(8,128)} %param.16) | copy-start | bytes 6148
  0.7 3.2 %copy-start = (bf16[2048,256]{1,0:T(8,128)(2,1)S(1)}, bf16[2048,256]{1,0:T(8,128)(2,1)}, u32[]{:S(2)}) copy-start(bf16[2048,256]{1,0:T(8,128)(2,1)} %q_next_ref.3) | copy-start | bytes 3145732
  0.7 3.2 %copy-start.1 = (bf16[2048,256]{1,0:T(8,128)(2,1)S(1)}, bf16[2048,256]{1,0:T(8,128)(2,1)}, u32[]{:S(2)}) copy-start(bf16[2048,256]{1,0:T(8,128)(2,1)} %do_next_ref.3) | copy-start | bytes 3145732
  0.7 3.2 %copy-start.2 = (bf16[2048,2]{0,1:T(2,128)(2,1)S(1)}, bf16[2048,2]{0,1:T(2,128)(2,1)}, u32[]{:S(2)}) copy-start(bf16[2048,2]{0,1:T(2,128)(2,1)} %param.14) | copy-start | bytes 24580
  0.7 3.2 %copy-start.3 = (bf16[2048,2]{0,1:T(2,128)(2,1)S(1)}, bf16[2048,2]{0,1:T(2,128)(2,1)}, u32[]{:S(2)}) copy-start(bf16[2048,2]{0,1:T(2,128)(2,1)} %param.15) | copy-start | bytes 24580
  3.9 5.1 %copy-start.4 = (bf16[1024,2,128]{2,1,0:T(2,128)(2,1)S(1)}, bf16[1024,2,128]{2,1,0:T(2,128)(2,1)}, u32[]{:S(2)}) copy-start(bf16[1024,2,128]{2,1,0:T(2,128)(2,1)} %get-tuple-element.7) | copy-start | bytes 1572868
  6.4 18.2 %collective-permute-start = (bf16[1024,256]{1,0:T(8,128)(2,1)S(1)}, bf16[1024,256]{1,0:T(8,128)(2,1)}, u32[]{:S(2)}, u32[]{:S(2)}) collective-permute-start(bf16[1024,256]{1,0:T(8,128)(2,1)S(1)} %attention_grads.2.refs_0_), channel_id=1, source_target_pairs={{0,1},{1,2},{2,3},{3,4},{4,5},{5,6},{6,7},{7,0},{8,9},{9,10},{10,1... | collective-permute-start | bytes 1572872 | tf_op jit(solution)/shard_map/ppermute | solution.py:196
  11.6 14.6 %collective-permute-start.3 = (bf16[1024,256]{1,0:T(8,128)(2,1)S(1)}, bf16[1024,256]{1,0:T(8,128)(2,1)}, u32[]{:S(2)}, u32[]{:S(2)}) collective-permute-start(bf16[1024,256]{1,0:T(8,128)(2,1)S(1)} %attention_grads.3.refs_1_), channel_id=1, source_target_pairs={{0,7},{1,0},{2,1},{3,2},{4,3},{5,4},{6,5},{7,6},{8,15},{9,8},{10,9... | collective-permute-start | bytes 1572872 | tf_op jit(solution)/shard_map/ppermute | solution.py:196
  15.6 20.3 %collective-permute-start.1 = (bf16[1024,256]{1,0:T(8,128)(2,1)S(1)}, bf16[1024,256]{1,0:T(8,128)(2,1)}, u32[]{:S(2)}, u32[]{:S(2)}) collective-permute-start(bf16[1024,256]{1,0:T(8,128)(2,1)S(1)} %attention_grads.3.refs_1_), channel_id=1, source_target_pairs={{0,1},{1,2},{2,3},{3,4},{4,5},{5,6},{6,7},{7,0},{8,9},{9,10},{10,1... | collective-permute-start | bytes 1572872 | tf_op jit(solution)/shard_map/ppermute | solution.py:196
  15.6 21.8 %collective-permute-start.2 = (bf16[1024,256]{1,0:T(8,128)(2,1)S(1)}, bf16[1024,256]{1,0:T(8,128)(2,1)}, u32[]{:S(2)}, u32[]{:S(2)}) collective-permute-start(bf16[1024,256]{1,0:T(8,128)(2,1)S(1)} %attention_grads.2.refs_0_), channel_id=1, source_target_pairs={{0,7},{1,0},{2,1},{3,2},{4,3},{5,4},{6,5},{7,6},{8,15},{9,8},{10,9... | collective-permute-start | bytes 1572872 | tf_op jit(solution)/shard_map/ppermute | solution.py:196
  24.7 22.5 %collective-permute-start.4 = (bf16[1024,256]{1,0:T(8,128)(2,1)}, bf16[1024,256]{1,0:T(8,128)(2,1)}, u32[]{:S(2)}, u32[]{:S(2)}) collective-permute-start(bf16[1024,256]{1,0:T(8,128)(2,1)} %collective-permute-done.refs_2_), channel_id=1, source_target_pairs={{0,1},{1,2},{2,3},{3,4},{4,5},{5,6},{6,7},{7,0},{8,9},{9,10},{10,1... | collective-permute-start | bytes 1572872 | tf_op jit(solution)/shard_map/ppermute | solution.py:196
  26.2 22.6 %collective-permute-start.7 = (bf16[1024,256]{1,0:T(8,128)(2,1)}, bf16[1024,256]{1,0:T(8,128)(2,1)}, u32[]{:S(2)}, u32[]{:S(2)}) collective-permute-start(bf16[1024,256]{1,0:T(8,128)(2,1)} %collective-permute-done.3.refs_5_), channel_id=1, source_target_pairs={{0,7},{1,0},{2,1},{3,2},{4,3},{5,4},{6,5},{7,6},{8,15},{9,8},{10,9... | collective-permute-start | bytes 1572872 | tf_op jit(solution)/shard_map/ppermute | solution.py:196
  35.9 30.7 %collective-permute-start.5 = (bf16[1024,256]{1,0:T(8,128)(2,1)}, bf16[1024,256]{1,0:T(8,128)(2,1)}, u32[]{:S(2)}, u32[]{:S(2)}) collective-permute-start(bf16[1024,256]{1,0:T(8,128)(2,1)} %collective-permute-done.1.refs_3_), channel_id=1, source_target_pairs={{0,1},{1,2},{2,3},{3,4},{4,5},{5,6},{6,7},{7,0},{8,9},{9,10},{10,1... | collective-permute-start | bytes 1572872 | tf_op jit(solution)/shard_map/ppermute | solution.py:196
  37.5 29.2 %collective-permute-start.6 = (bf16[1024,256]{1,0:T(8,128)(2,1)}, bf16[1024,256]{1,0:T(8,128)(2,1)}, u32[]{:S(2)}, u32[]{:S(2)}) collective-permute-start(bf16[1024,256]{1,0:T(8,128)(2,1)} %collective-permute-done.2.refs_4_), channel_id=1, source_target_pairs={{0,7},{1,0},{2,1},{3,2},{4,3},{5,4},{6,5},{7,6},{8,15},{9,8},{10,9... | collective-permute-start | bytes 1572872 | tf_op jit(solution)/shard_map/ppermute | solution.py:196
  47.1 22.5 %collective-permute-start.8 = (bf16[1024,256]{1,0:T(8,128)(2,1)}, bf16[1024,256]{1,0:T(8,128)(2,1)}, u32[]{:S(2)}, u32[]{:S(2)}) collective-permute-start(bf16[1024,256]{1,0:T(8,128)(2,1)} %collective-permute-done.4.refs_0_), channel_id=1, source_target_pairs={{0,1},{1,2},{2,3},{3,4},{4,5},{5,6},{6,7},{7,0},{8,9},{9,10},{10,1... | collective-permute-start | bytes 1572872 | tf_op jit(solution)/shard_map/ppermute | solution.py:196
  48.8 22.5 %collective-permute-start.11 = (bf16[1024,256]{1,0:T(8,128)(2,1)}, bf16[1024,256]{1,0:T(8,128)(2,1)}, u32[]{:S(2)}, u32[]{:S(2)}) collective-permute-start(bf16[1024,256]{1,0:T(8,128)(2,1)} %collective-permute-done.7.refs_3_), channel_id=1, source_target_pairs={{0,7},{1,0},{2,1},{3,2},{4,3},{5,4},{6,5},{7,6},{8,15},{9,8},{10,9... | collective-permute-start | bytes 1572872 | tf_op jit(solution)/shard_map/ppermute | solution.py:196
  56.4 24.4 %all-to-all-start = ((bf16[32,16,768]{2,1,0:T(8,128)(2,1)}), bf16[32,16,768]{2,1,0:T(8,128)(2,1)}, u32[]{:S(2)}, u32[]{:S(2)}) async-start(bf16[32,16,768]{2,1,0:T(8,128)(2,1)} %bitcast.5), calls=%async_computation | async-start | bytes 1572864 | tf_op jit(solution)/shard_map/all_to_all | solution.py:202
  66.6 21.8 %collective-permute-start.9 = (bf16[1024,256]{1,0:T(8,128)(2,1)}, bf16[1024,256]{1,0:T(8,128)(2,1)S(1)}, u32[]{:S(2)}, u32[]{:S(2)}) collective-permute-start(bf16[1024,256]{1,0:T(8,128)(2,1)} %collective-permute-done.5.refs_1_), channel_id=1, source_target_pairs={{0,1},{1,2},{2,3},{3,4},{4,5},{5,6},{6,7},{7,0},{8,9},{9,10},{10,1... | collective-permute-start | bytes 1572872 | tf_op jit(solution)/shard_map/ppermute | solution.py:196
  66.7 21.7 %collective-permute-start.10 = (bf16[1024,256]{1,0:T(8,128)(2,1)}, bf16[1024,256]{1,0:T(8,128)(2,1)S(1)}, u32[]{:S(2)}, u32[]{:S(2)}) collective-permute-start(bf16[1024,256]{1,0:T(8,128)(2,1)} %collective-permute-done.6.refs_2_), channel_id=1, source_target_pairs={{0,7},{1,0},{2,1},{3,2},{4,3},{5,4},{6,5},{7,6},{8,15},{9,8},{10,9... | collective-permute-start | bytes 1572872 | tf_op jit(solution)/shard_map/ppermute | solution.py:196
  69.6 23.0 %collective-permute-start.12 = (bf16[1024,256]{1,0:T(8,128)(2,1)}, bf16[1024,256]{1,0:T(8,128)(2,1)}, u32[]{:S(2)}, u32[]{:S(2)}) collective-permute-start(bf16[1024,256]{1,0:T(8,128)(2,1)} %collective-permute-done.8.refs_0_), channel_id=1, source_target_pairs={{0,1},{1,2},{2,3},{3,4},{4,5},{5,6},{6,7},{7,0},{8,9},{9,10},{10,1... | collective-permute-start | bytes 1572872 | tf_op jit(solution)/shard_map/ppermute | solution.py:196
  71.3 22.5 %collective-permute-start.13 = (bf16[1024,256]{1,0:T(8,128)(2,1)}, bf16[1024,256]{1,0:T(8,128)(2,1)}, u32[]{:S(2)}, u32[]{:S(2)}) collective-permute-start(bf16[1024,256]{1,0:T(8,128)(2,1)} %collective-permute-done.11.refs_3_), channel_id=1, source_target_pairs={{0,7},{1,0},{2,1},{3,2},{4,3},{5,4},{6,5},{7,6},{8,15},{9,8},{10,9... | collective-permute-start | bytes 1572872 | tf_op jit(solution)/shard_map/ppermute | solution.py:196
  80.9 19.2 %all-to-all-start.1 = ((bf16[32,16,512]{2,1,0:T(8,128)(2,1)}), bf16[32,16,512]{2,1,0:T(8,128)(2,1)}, u32[]{:S(2)}, u32[]{:S(2)}) async-start(bf16[32,16,512]{2,1,0:T(8,128)(2,1)} %bitcast.6), calls=%async_computation.1 | async-start | bytes 1048576 | tf_op jit(solution)/shard_map/all_to_all | solution.py:202
  100.1 20.8 %all-to-all-start.2 = ((bf16[32,16,768]{2,1,0:T(8,128)(2,1)}), bf16[32,16,768]{2,1,0:T(8,128)(2,1)S(1)}, u32[]{:S(2)}, u32[]{:S(2)}) async-start(bf16[32,16,768]{2,1,0:T(8,128)(2,1)} %bitcast.7), calls=%async_computation.2 | async-start | bytes 1572864 | tf_op jit(solution)/shard_map/all_to_all | solution.py:202
  106.6 39.0 %copy-start.8 = (f32[2,8]{1,0:T(2,128)S(1)}, f32[2,8]{1,0:T(2,128)}, u32[]{:S(2)}) copy-start(f32[2,8]{1,0:T(2,128)} %param.19) | copy-start | bytes 196
  106.6 39.6 %copy-start.5 = (f32[16,2,1024]{2,1,0:T(2,128)S(1)}, f32[16,2,1024]{2,1,0:T(2,128)}, u32[]{:S(2)}) copy-start(f32[16,2,1024]{2,1,0:T(2,128)} %param.18) | copy-start | bytes 393220
  135.7 9.9 %all-to-all-start.4 = ((f32[16,2,8]{2,1,0:T(2,128)}), f32[16,2,8]{2,1,0:T(2,128)S(1)}, u32[]{:S(2)}, u32[]{:S(2)}) async-start(f32[16,2,8]{2,1,0:T(2,128)} %broadcast_in_dim.5), calls=%async_computation.4 | async-start | bytes 32768 | tf_op jit(solution)/shard_map/all_to_all | solution.py:208
